TPU v7x, 256 devices: a whole 4x4x8 slice. The times are simulated.
256 devices in a mesh: tm: 8 (over x_lo, y), freq: 32 (over x_hi, z, core).
Axes of the slice: x: 4 (x_hi: 2, x_lo: 2; x = x_hi * 2 + x_lo), y: 4, z: 8, core: 2. Of those that a mesh axis runs over, the one named last changes fastest.
Arguments:
- voltages: bfloat16 [1024, 196608], P('freq', 'tm'), may hold values from -6 to 6
- window: float32 [8, 256], replicated, may hold values from -2 to 2
Outputs:
- visibilities: float32 [2, 128, 1024, 1024], P(None, 'freq', 'tm')
All inputs are finite; a program needn't handle non-finite values.
Results may differ from a plain program's by a relative error of at most 0.0031.
Values may be sent and summed in bfloat16 or wider, within the bound.
A program may use at most 128 MiB of HBM per device.

v0:
```python
import math

import jax
import jax.numpy as jnp
from jax import lax
from jax.sharding import PartitionSpec as P


def from_behind(value, axis, steps):
    count = lax.axis_size(axis)
    first, last = (max(0, -steps), min(count, count - steps))
    return lax.ppermute(value, axis, [(source, source + steps) for source in range(first, last)])


def dft_table(length, channels):
    sample = jnp.arange(length, dtype=jnp.int32)[:, None]
    channel = jnp.arange(channels, dtype=jnp.int32)[None, :]
    phase = (sample * channel % length).astype(jnp.float32) * (2.0 * math.pi / length)
    return jnp.concatenate([jnp.cos(phase), -jnp.sin(phase)], axis=1) * length ** (-0.5)


def gram_rows(signal, row_start, row_count):
    left = lax.dynamic_slice_in_dim(signal, row_start, row_count, 0)
    paired = jnp.stack([-signal[:, :, 1, :], signal[:, :, 0, :]], axis=2)
    real_part = jnp.einsum("asrc,bsrc->cab", left, signal, preferred_element_type=jnp.float32)
    imag_part = jnp.einsum("asrc,bsrc->cab", left, paired, preferred_element_type=jnp.float32)
    return (real_part, imag_part)


def local(voltages, window):
    taps = window.shape[0]
    period = window.shape[1]
    channels = period // 2
    antennas_here = voltages.shape[0]
    blocks = voltages.reshape(antennas_here, -1, period)
    spec_here = blocks.shape[1]
    history = from_behind(blocks[:, spec_here - (taps - 1) :, :], "tm", 1)
    joined = jnp.concatenate([history, blocks], axis=1).astype(jnp.float32)
    filtered = jnp.zeros((antennas_here, spec_here, period), jnp.float32)
    for tap_index in range(taps):
        filtered = (
            filtered
            + window[tap_index][None, None, :] * joined[:, tap_index : tap_index + spec_here, :]
        )
    spectra = jnp.dot(
        filtered.reshape(-1, period), dft_table(period, channels), precision=lax.Precision.HIGHEST
    )
    spectra = spectra.reshape(antennas_here, spec_here, 2, channels).astype(jnp.bfloat16)
    antennas_all = antennas_here * lax.axis_size("freq")
    row_count = antennas_all // lax.axis_size("tm")
    row_start = lax.axis_index("tm") * row_count
    spectra_total = spec_here * lax.axis_size("tm")
    whole = lax.all_gather(spectra, "tm", axis=1, tiled=True)
    turned = lax.all_to_all(whole, "freq", split_axis=3, concat_axis=0, tiled=True)
    real_part, imag_part = gram_rows(turned, row_start, row_count)
    return jnp.stack([real_part, imag_part]) * spectra_total ** (-0.5)


def solution(mesh):
    return jax.shard_map(
        local,
        mesh=mesh,
        in_specs=(P("freq", "tm"), P()),
        out_specs=P(None, "freq", "tm", None),
        check_vma=False,
    )
```

profile of v0, /device:TPU:24, one launch (start us, length us, event | category | flops | bytes accessed | tf_op | source)
XLA Modules:
  0.0 520.8 jit_solution(16650168149202176707)
XLA Ops:
  6.5 0.0 copy-start.1
  6.5 0.0 all-gather.2.cloned.1.call-start
  6.5 1.8 copy.12
  8.4 3.1 collective-permute-start
  11.4 0.5 sine_negate_fusion
  12.0 0.0 copy-done.1
  12.0 3.5 collective-permute-done
  15.5 0.4 maximum_convert_fusion
  15.9 6.4 %fusion.20 = bf16[32,96,2,128]{3,1,2,0:T(8,128)(2,1)} fusion(f32[2,128,256,1]{2,1,0,3:T(8,128)S(1)} %bitcast.43, f32[32,103,256]{2,1,0:T(8,128)S(1)} %maximum_convert_fusion, f32[256]{0:T(256)S(1)} %bitcast.50, f32[256]{0:T(256)S(1)} %bitcast.51, f32[256]{0:T(256)S(1)} %bitcast.45, f32[256]{0:T(256)S(1)} %bitcast.46, f32[256]{0:T(256)S(1)} %bitcast.47, ...), kind=kOutput, calls=%fused_computation.24 | convolution fusion | flops 2428502016 | bytes 27009024 | tf_op jit(solution)/shard_map/dot_general | solution.py:45
  22.3 0.0 all-gather.2.cloned.1.call-update
  22.4 134.4 %all-gather.2.cloned.1.call-done = bf16[32,768,2,128]{3,1,2,0:T(8,128)(2,1)} async-done(((bf16[32,96,2,128]{3,1,2,0:T(8,128)(2,1)}), bf16[32,768,2,128]{3,1,2,0:T(8,128)(2,1)}) %all-gather.2.cloned.1.call-update) | async-done | bytes 12582928 | tf_op jit(solution)/shard_map/all_gather | solution.py:53
  156.7 31.6 %copy.6 = bf16[32,768,2,128]{1,2,0,3:T(2,128)(2,1)} copy(bf16[32,768,2,128]{3,1,2,0:T(8,128)(2,1)} %all-gather.2.cloned.1.call-done) | data formatting | bytes 25165824 | tf_op jit(solution)/shard_map/all_gather | solution.py:53
  188.3 9.6 %all-to-all-start = ((bf16[32,768,2,128]{1,2,0,3:T(2,128)(2,1)}), bf16[32,768,2,128]{1,2,0,3:T(2,128)(2,1)}, u32[]{:S(2)}, u32[]{:S(2)}) async-start(bf16[32,768,2,128]{1,2,0,3:T(2,128)(2,1)} %copy.6), calls=%async_computation | async-start | bytes 25165824 | tf_op jit(solution)/shard_map/all_to_all | solution.py:54
  198.0 279.4 %all-to-all-done = bf16[32,768,2,128]{1,2,0,3:T(2,128)(2,1)} async-done(((bf16[32,768,2,128]{1,2,0,3:T(2,128)(2,1)}), bf16[32,768,2,128]{1,2,0,3:T(2,128)(2,1)}, u32[]{:S(2)}, u32[]{:S(2)}) %all-to-all-start) | async-done | bytes 12582944 | tf_op jit(solution)/shard_map/all_to_all | solution.py:54
  477.4 7.7 %copy.7 = bf16[32,768,2,128]{1,0,3,2:T(8,128)(2,1)S(1)} copy(bf16[32,768,2,128]{1,2,0,3:T(2,128)(2,1)} %all-to-all-done) | data formatting | bytes 25165824 | tf_op jit(solution)/shard_map/all_to_all | solution.py:54
  485.0 2.4 copy.8
  487.4 0.0 copy-start
  487.4 4.5 copy-done
  491.9 3.4 slice_negate_fusion
  495.3 9.1 %convolution_bitcast_fusion = f32[1,4,128,1024]{3,2,1,0:T(8,128)S(1)} fusion(bf16[1024,768,2,4]{1,0,2,3:T(8,128)(2,1)} %bitcast.37, s32[]{:T(128)S(6)} %select_n.13), kind=kOutput, calls=%fused_computation.26 | convolution fusion | flops 1610612736 | bytes 16252932 | tf_op jit(solution)/shard_map/asrc,bsrc->cab/dot_general | solution.py:25
  504.5 6.9 %fusion.23 = f32[1,4,128,1024]{3,2,1,0:T(8,128)S(1)} fusion(bf16[1024,768,1,4]{1,0,2,3:T(8,128)(2,1)} %get-tuple-element.6, bf16[1024,768,1,4]{1,0,2,3:T(8,128)(2,1)S(1)} %get-tuple-element.5, bf16[1024,768,2,4]{1,0,2,3:T(8,128)(2,1)} %bitcast.38, s32[]{:T(128)S(6)} %select_n.13), kind=kOutput, calls=%fused_computation.25 | convolution fusion | flops 1616904192 | bytes 16252932 | tf_op jit(solution)/shard_map/asrc,bsrc->cab/dot_general | solution.py:26
  511.4 2.5 maximum_multiply_fusion
  (3 shorter events, 0.1 us)
Async XLA Ops:
  6.5 5.4 %copy-start.1 = (f32[8,256]{1,0:T(8,128)S(1)}, f32[8,256]{1,0:T(8,128)}, u32[]{:S(2)}) copy-start(f32[8,256]{1,0:T(8,128)} %param.3) | copy-start | bytes 24580
  6.5 150.2 %all-gather.2.cloned.1.call-start = ((), (), s32[]{:S(2)}) async-start(), calls=%async_computation.1 | async-start | bytes 14155776 | tf_op jit(solution)/shard_map/all_gather | solution.py:53
  8.4 7.1 %collective-permute-start = (bf16[32,7,256]{2,1,0:T(8,128)(2,1)S(1)}, bf16[32,7,256]{2,1,0:T(8,128)(2,1)S(1)}, u32[]{:S(2)}, u32[]{:S(2)}) collective-permute-start(bf16[32,7,256]{2,1,0:T(8,128)(2,1)S(1)} %slice.76), channel_id=1, source_target_pairs={{0,32},{32,64},{64,96},{96,128},{128,160},{160,192},{192,224},{1,3... | collective-permute-start | bytes 344072 | tf_op jit(solution)/shard_map/ppermute | solution.py:12
  188.3 289.0 %all-to-all-start = ((bf16[32,768,2,128]{1,2,0,3:T(2,128)(2,1)}), bf16[32,768,2,128]{1,2,0,3:T(2,128)(2,1)}, u32[]{:S(2)}, u32[]{:S(2)}) async-start(bf16[32,768,2,128]{1,2,0,3:T(2,128)(2,1)} %copy.6), calls=%async_computation | async-start | bytes 25165824 | tf_op jit(solution)/shard_map/all_to_all | solution.py:54
  487.4 4.5 copy-start
Sparse Core Ops, SparseCore 0:
  22.5 134.2 all-gather.1
where the time goes:
time: 524 us; the launch traced here: 521 us
  waiting for transfers between devices  417 us (80%)
  local copies, waits for them, and re-layouts  48 us (9%)
  matrix products  22.5 us (4%)
  between operations  13.5 us (3%)
  starting transfers between devices  12.7 us (2%)
  other arithmetic  6.87 us (1%)
    all_to_all x1, waiting for transfers between devices, local(): lax.all_to_all(whole, 'freq', split_axis=3, concat_axis=0, tiled=True)  279 us
    all_gather x1, waiting for transfers between devices, local(): whole = lax.all_gather(spectra, 'tm', axis=1, tiled=True)  134 us
    all_gather x1, local copies, waits for them, and re-layouts, local(): whole = lax.all_gather(spectra, 'tm', axis=1, tiled=True)  31.6 us
  transfers between devices with their start and end apart: 3, of which 3 were waited for; matrix products, arithmetic and copies ran while one was open for 0% of the time, Pallas kernels for 0%

commit v1 on v0

v1 whole, which is shorter than its diff:
```python
import functools
import math

import jax
import jax.numpy as jnp
from jax import lax
from jax.experimental import pallas as pl
from jax.experimental.pallas import tpu as pltpu
from jax.sharding import PartitionSpec as P

MESH = pl.DeviceIdType.MESH
LANES = 128


def from_behind(value, axis, steps):
    count = lax.axis_size(axis)
    first, last = (max(0, -steps), min(count, count - steps))
    return lax.ppermute(value, axis, [(source, source + steps) for source in range(first, last)])


def dft_table(length, channels):
    sample = jnp.arange(length, dtype=jnp.int32)[:, None]
    channel = jnp.arange(channels, dtype=jnp.int32)[None, :]
    phase = (sample * channel % length).astype(jnp.float32) * (2.0 * math.pi / length)
    return jnp.concatenate([jnp.cos(phase), -jnp.sin(phase)], axis=1) * length ** (-0.5)


def channelize(voltages, window):
    taps, period = window.shape
    channels = period // 2
    antennas = voltages.shape[0]
    blocks = voltages.reshape(antennas, -1, period)
    spec_here = blocks.shape[1]
    history = from_behind(blocks[:, spec_here - (taps - 1) :, :], "tm", 1)
    joined = jnp.concatenate([history, blocks], axis=1).astype(jnp.float32)
    filtered = jnp.zeros((antennas, spec_here, period), jnp.float32)
    for k in range(taps):
        filtered = filtered + window[k][None, None, :] * joined[:, k : k + spec_here, :]
    spectra = jnp.dot(
        filtered.reshape(-1, period), dft_table(period, channels), precision=lax.Precision.HIGHEST
    )
    return spectra.reshape(antennas, spec_here, 2, channels).astype(jnp.bfloat16)


def pack(spectra):
    antennas, spec, _, channels = spectra.shape
    main = 2 * spec // 3
    first = spectra[:, :main].transpose(3, 0, 2, 1).reshape(channels, antennas, LANES)
    rest = spectra[:, main:].reshape(2, antennas // 2, spec - main, 2, channels)
    rest = rest.transpose(4, 1, 0, 3, 2).reshape(channels, antennas // 2, LANES)
    return jnp.concatenate([first, rest], axis=1)


def correlate_kernel(
    tms, groups, scale, s_ref, r_ref, x_ref, full, swapped, outs, send1, recv1, send2, recv2, sib
):
    t, f = lax.axis_index("tm"), lax.axis_index("freq")
    g, k = f // 2, f % 2
    half = tms // 2
    peers = tms * groups
    rows = s_ref.shape[1]
    ants = 2 * rows // 3
    sibling = (t, 2 * g + 1 - k)

    barrier = pltpu.get_barrier_semaphore()

    def peer(i):
        return lax.rem(t + i // groups, tms), lax.rem(g + i % groups, groups)

    def greet(i, _):
        tt, gg = peer(i)
        pl.semaphore_signal(barrier, inc=1, device_id=(tt, 2 * gg + k), device_id_type=MESH)
        return 0

    lax.fori_loop(1, peers, greet, 0)
    pl.semaphore_signal(barrier, inc=1, device_id=sibling, device_id_type=MESH)

    def greet_source(j, _):
        tt = half * k + j

        @pl.when((tt != t) | (k != t // half))
        def _():
            pl.semaphore_signal(
                barrier, inc=1, device_id=(tt, 2 * g + t // half), device_id_type=MESH
            )

        return 0

    lax.fori_loop(0, half, greet_source, 0)
    pl.semaphore_wait(barrier, peers + half - jnp.where(k == t // half, 1, 0))

    def send_block(i, _):
        tt, gg = peer(i)
        pltpu.make_async_remote_copy(
            src_ref=s_ref.at[gg * tms + tt],
            dst_ref=x_ref.at[k, t, g],
            send_sem=send1,
            recv_sem=recv1,
            device_id=(tt, 2 * gg + k),
            device_id_type=MESH,
        ).start()
        return 0

    lax.fori_loop(1, peers, send_block, 0)
    pltpu.make_async_copy(s_ref.at[g * tms + t], x_ref.at[k, t, g], recv1).start()
    pltpu.make_async_copy(x_ref.at[k], x_ref.at[k], recv1).wait()

    share = pltpu.make_async_remote_copy(
        src_ref=x_ref.at[k],
        dst_ref=x_ref.at[k],
        send_sem=sib.at[0],
        recv_sem=sib.at[1],
        device_id=sibling,
        device_id_type=MESH,
    )
    share.start()
    share.wait_recv()

    lane = lax.broadcasted_iota(jnp.int32, (rows - ants, LANES), 1)
    low = lane < LANES // 2
    wide = tms * LANES

    def assemble(i, _):
        gg, kk = i // 2, i % 2
        base = pl.multiple_of(i * ants, ants)
        for tt in range(tms):
            full[pl.ds(base, ants), tt * LANES : (tt + 1) * LANES] = x_ref[kk, tt, gg, :ants, :]
        for tt in range(0, tms, 2):
            h0 = x_ref[kk, tt, gg, ants:, :].astype(jnp.float32)
            h1 = x_ref[kk, tt + 1, gg, ants:, :].astype(jnp.float32)
            top = jnp.where(low, h0, pltpu.roll(h1, LANES // 2, 1))
            bottom = jnp.where(low, pltpu.roll(h0, LANES // 2, 1), h1)
            at = wide + tt // 2 * LANES
            full[pl.ds(base, ants // 2), at : at + LANES] = top.astype(jnp.bfloat16)
            full[pl.ds(base + ants // 2, ants // 2), at : at + LANES] = bottom.astype(jnp.bfloat16)
        return 0

    lax.fori_loop(0, 2 * groups, assemble, 0)

    own = full.shape[0] // 2
    own_base = pl.multiple_of(k * own, own)
    step = 16
    lane = lax.broadcasted_iota(jnp.int32, (step, LANES), 1)
    low = lane < LANES // 2
    quarter = lane % (LANES // 2) < LANES // 4

    def swap(i, _):
        at = pl.multiple_of(i * step, step)
        for tile in range(full.shape[1] // LANES):
            cols = slice(tile * LANES, (tile + 1) * LANES)
            v = full[pl.ds(own_base + at, step), cols].astype(jnp.float32)
            if tile < tms:
                v = pltpu.roll(v, LANES // 2, 1)
                v = jnp.where(low, v, -v)
            else:
                v = jnp.where(
                    quarter, pltpu.roll(v, LANES - LANES // 4, 1), -pltpu.roll(v, LANES // 4, 1)
                )
            swapped[pl.ds(at, step), cols] = v.astype(jnp.bfloat16)
        return 0

    lax.fori_loop(0, own // step, swap, 0)

    tile = 256
    row_count = own // half
    slot = t % half

    def columns(n, _):
        at = pl.multiple_of(n * tile, tile)
        right = full[pl.ds(at, tile), :]
        dims = (((1,), (1,)), ((), ()))
        for part, left in enumerate((full.at[pl.ds(own_base, own), :], swapped)):
            value = lax.dot_general(
                left[...], right, dims, preferred_element_type=jnp.float32
            )
            value = (value * scale).astype(jnp.bfloat16)
            outs[:, part, :, pl.ds(at, tile)] = value.reshape(half, row_count, tile)
        for i in range(half):
            target = (half * k + i, 2 * g + t // half)
            here = (t == half * k + i) & (k == t // half)
            src = outs.at[i, :, :, pl.ds(at, tile)]
            dst = r_ref.at[:, slot, :, pl.ds(at, tile)]

            @pl.when(here)
            def _():
                pltpu.make_async_copy(src, dst, recv2).start()

            @pl.when(jnp.logical_not(here))
            def _():
                pltpu.make_async_remote_copy(
                    src_ref=src,
                    dst_ref=dst,
                    send_sem=send2,
                    recv_sem=recv2,
                    device_id=target,
                    device_id_type=MESH,
                ).start()

        return 0

    lax.fori_loop(0, full.shape[0] // tile, columns, 0)
    pltpu.make_async_copy(r_ref, r_ref, recv2).wait()

    share.wait_send()
    sent = s_ref.at[pl.ds(0, peers - 1)]
    pltpu.make_async_copy(sent, sent, send1).wait()

    @pl.when(k == t // half)
    def _():
        part = outs.at[pl.ds(0, half - 1)]
        pltpu.make_async_copy(part, part, send2).wait()

    @pl.when(k != t // half)
    def _():
        pltpu.make_async_copy(outs, outs, send2).wait()


def local(voltages, window):
    tms, freqs = lax.axis_size("tm"), lax.axis_size("freq")
    groups = freqs // 2
    half = tms // 2
    spectra = channelize(voltages, window)
    antennas, spec_here, _, channels = spectra.shape
    assert channels == tms * groups
    blocks = pack(spectra)
    rows = blocks.shape[1]
    total = antennas * freqs
    row_count = total // tms
    depth = 2 * spec_here * tms
    result = pl.pallas_call(
        functools.partial(correlate_kernel, tms, groups, (spec_here * tms) ** (-0.5)),
        out_shape=jax.ShapeDtypeStruct((2, half, row_count, total), jnp.bfloat16),
        in_specs=[pl.BlockSpec(memory_space=pltpu.VMEM)],
        out_specs=pl.BlockSpec(memory_space=pl.ANY),
        scratch_shapes=[
            pltpu.VMEM((2, tms, groups, rows, LANES), jnp.bfloat16),
            pltpu.VMEM((total, depth), jnp.bfloat16),
            pltpu.VMEM((total // 2, depth), jnp.bfloat16),
            pltpu.VMEM((half, 2, row_count, total), jnp.bfloat16),
            pltpu.SemaphoreType.DMA,
            pltpu.SemaphoreType.DMA,
            pltpu.SemaphoreType.DMA,
            pltpu.SemaphoreType.DMA,
            pltpu.SemaphoreType.DMA((2,)),
        ],
        compiler_params=pltpu.CompilerParams(
            collective_id=0, has_side_effects=True, vmem_limit_bytes=40 << 20
        ),
        cost_estimate=pl.CostEstimate(
            flops=2 * 2 * (total // 2) * total * depth, bytes_accessed=8 << 20, transcendentals=0
        ),
    )(blocks)
    return result.astype(jnp.float32)


def solution(mesh):
    return jax.shard_map(
        local,
        mesh=mesh,
        in_specs=(P("freq", "tm"), P()),
        out_specs=P(None, "freq", "tm", None),
        check_vma=False,
    )
```

time: 524 us -> 105 us (0.20)
  the two profiles are of different devices: /device:TPU:24 before, /device:TPU:26 now
where the time goes in v1:
time: 105 us
  Pallas kernels  86.3 us (82%)
  matrix products  5.31 us (5%)
  waiting for transfers between devices  5.24 us (5%)
  other arithmetic  3.55 us (3%)
  local copies, waits for them, and re-layouts  3.42 us (3%)
  starting transfers between devices  1.29 us (1%)
    pallas_call x1, Pallas kernels, local(): pl.pallas_call(functools.partial(correlate_kernel, tms, groups, (spec_her...  86.3 us
    dot_general x1, matrix products, channelize(): jnp.dot(filtered.reshape(-1, period), dft_table(period, channels), precis...  5.31 us
    ppermute x1, waiting for transfers between devices, from_behind(): lax.ppermute(value, axis, [(source, source + steps) for source in range(f...  5.24 us
    convert_element_type x1, other arithmetic, local(): return result.astype(jnp.float32)  2.48 us
  transfers between devices with their start and end apart: 1, of which 1 were waited for; matrix products, arithmetic and copies ran while one was open for 1% of the time, Pallas kernels for 0%

profile of v1, /device:TPU:26, one launch (start us, length us, event | category | flops | bytes accessed | tf_op | source)
XLA Modules:
  0.0 105.3 jit_solution(11882758320298012269)
XLA Ops:
  0.0 0.0 copy-start
  0.0 1.8 %copy.9 = bf16[4,8,96,256]{3,2,1,0:T(8,128)(2,1)S(1)} copy(bf16[4,8,96,256]{3,1,2,0:T(8,128)(2,1)} %bitcast.35) | data formatting | bytes 3145728
  1.8 1.3 %collective-permute-start = (bf16[32,7,256]{2,1,0:T(8,128)(2,1)S(1)}, bf16[32,7,256]{2,1,0:T(8,128)(2,1)S(1)}, u32[]{:S(2)}, u32[]{:S(2)}) collective-permute-start(bf16[32,7,256]{2,1,0:T(8,128)(2,1)S(1)} %slice.76), channel_id=1, source_target_pairs={{0,32},{32,64},{64,96},{96,128},{128,160},{160,192},{192,224},{1,3... | collective-permute-start | bytes 344072 | tf_op jit(solution)/shard_map/ppermute | solution.py:18
  3.1 0.5 sine_negate_fusion
  3.7 0.0 copy-done
  3.7 5.2 %collective-permute-done = bf16[32,7,256]{2,1,0:T(8,128)(2,1)S(1)} collective-permute-done((bf16[32,7,256]{2,1,0:T(8,128)(2,1)S(1)}, bf16[32,7,256]{2,1,0:T(8,128)(2,1)S(1)}, u32[]{:S(2)}, u32[]{:S(2)}) %collective-permute-start) | collective-permute-done | bytes 114720 | tf_op jit(solution)/shard_map/ppermute | solution.py:18
  9.0 0.4 maximum_convert_fusion
  9.4 5.3 %fusion.16 = bf16[32,96,2,128]{3,1,2,0:T(8,128)(2,1)S(1)} fusion(f32[2,128,256,1]{2,1,0,3:T(8,128)S(1)} %bitcast.36, f32[32,103,256]{2,1,0:T(8,128)S(1)} %maximum_convert_fusion, f32[256]{0:T(256)S(1)} %bitcast.43, f32[256]{0:T(256)S(1)} %bitcast.44, f32[256]{0:T(256)S(1)} %bitcast.38, f32[256]{0:T(256)S(1)} %bitcast.39, f32[256]{0:T(256)S(1)} %bitcast.40, ...), kind=kOutput, calls=%fused_computation.18 | convolution fusion | flops 2428502016 | bytes 27009024 | tf_op jit(solution)/shard_map/dot_general | solution.py:39
  14.7 0.1 slice.85
  14.9 1.0 copy.6
  15.9 0.4 copy.7
  16.3 0.1 pad_maximum_fusion.s_ref
  16.4 86.3 %shard_map.28 = bf16[2,4,128,1024]{3,2,1,0:T(8,128)(2,1)S(1)} custom-call(bf16[128,48,128]{2,1,0:T(8,128)(2,1)S(1)} %pad_maximum_fusion.s_ref), custom_call_target="tpu_custom_call" | custom-call | flops 3221225472 | bytes 8388608 | tf_op jit(solution)/shard_map/pallas_call | solution.py:230
  102.8 2.5 %convert_element_type.17 = f32[2,4,128,1024]{3,2,1,0:T(8,128)} convert(bf16[2,4,128,1024]{3,2,1,0:T(8,128)(2,1)S(1)} %shard_map.28) | non-fusion elementwise | flops 1048576 | bytes 6291456 | tf_op jit(solution)/shard_map/convert_element_type | solution.py:253
  (5 shorter events, 0.1 us)
Async XLA Ops:
  0.0 3.7 %copy-start = (f32[8,256]{1,0:T(8,128)S(1)}, f32[8,256]{1,0:T(8,128)}, u32[]{:S(2)}) copy-start(f32[8,256]{1,0:T(8,128)} %param.3) | copy-start | bytes 24580
  1.8 7.1 %collective-permute-start = (bf16[32,7,256]{2,1,0:T(8,128)(2,1)S(1)}, bf16[32,7,256]{2,1,0:T(8,128)(2,1)S(1)}, u32[]{:S(2)}, u32[]{:S(2)}) collective-permute-start(bf16[32,7,256]{2,1,0:T(8,128)(2,1)S(1)} %slice.76), channel_id=1, source_target_pairs={{0,32},{32,64},{64,96},{96,128},{128,160},{160,192},{192,224},{1,3... | collective-permute-start | bytes 344072 | tf_op jit(solution)/shard_map/ppermute | solution.py:18

commit v2 on v1

v2 whole, which is shorter than its diff:
```python
import functools
import math

import jax
import jax.numpy as jnp
from jax import lax
from jax.experimental import pallas as pl
from jax.experimental.pallas import tpu as pltpu
from jax.sharding import PartitionSpec as P

MESH = pl.DeviceIdType.MESH
LANES = 128
LEAD = 4


def from_behind(value, axis, steps):
    count = lax.axis_size(axis)
    first, last = (max(0, -steps), min(count, count - steps))
    return lax.ppermute(value, axis, [(source, source + steps) for source in range(first, last)])


def dft_table(length, channels):
    sample = jnp.arange(length, dtype=jnp.int32)[:, None]
    channel = jnp.arange(channels, dtype=jnp.int32)[None, :]
    phase = (sample * channel % length).astype(jnp.float32) * (2.0 * math.pi / length)
    return jnp.concatenate([jnp.cos(phase), -jnp.sin(phase)], axis=1) * length ** (-0.5)


def channelize(voltages, window):
    taps, period = window.shape
    channels = period // 2
    antennas = voltages.shape[0]
    blocks = voltages.reshape(antennas, -1, period)
    spec_here = blocks.shape[1]
    history = from_behind(blocks[:, spec_here - (taps - 1) :, :], "tm", 1)
    joined = jnp.concatenate([history, blocks], axis=1).astype(jnp.float32)
    filtered = jnp.zeros((antennas, spec_here, period), jnp.float32)
    for k in range(taps):
        filtered = filtered + window[k][None, None, :] * joined[:, k : k + spec_here, :]
    spectra = jnp.dot(
        filtered.reshape(-1, period), dft_table(period, channels), precision=lax.Precision.HIGHEST
    )
    return spectra.reshape(antennas, spec_here, 2, channels).astype(jnp.bfloat16)


def pack(spectra):
    antennas, spec, _, channels = spectra.shape
    main = 2 * spec // 3
    first = spectra[:, :main].transpose(3, 0, 2, 1).reshape(channels, antennas, LANES)
    rest = spectra[:, main:].reshape(2, antennas // 2, spec - main, 2, channels)
    rest = rest.transpose(4, 1, 0, 3, 2).reshape(channels, antennas // 2, LANES)
    return jnp.concatenate([first, rest], axis=1)


def correlate_kernel(
    tms, groups, scale, s_ref, r_ref, x_ref, right, left, outs, send1, recv1, send2, recv2, send3, recv3
):
    t, f = lax.axis_index("tm"), lax.axis_index("freq")
    g, k = f // 2, f % 2
    half = tms // 2
    peers = tms * groups
    rows = s_ref.shape[1]
    ants = 2 * rows // 3
    sibling = (t, 2 * g + 1 - k)
    mine = g // 2 % half
    first_part = lax.rem(mine + t, half)

    barrier = pltpu.get_barrier_semaphore()

    def greet(i, _):
        tt, gg = lax.rem(t + i // groups, tms), lax.rem(g + i % groups, groups)
        pl.semaphore_signal(barrier, inc=1, device_id=(tt, 2 * gg + k), device_id_type=MESH)
        return 0

    lax.fori_loop(1, peers, greet, 0)
    pl.semaphore_signal(barrier, inc=1, device_id=sibling, device_id_type=MESH)

    def greet_source(j, _):
        tt = half * k + j

        @pl.when((tt != t) | (k != t // half))
        def _():
            pl.semaphore_signal(
                barrier, inc=1, device_id=(tt, 2 * g + t // half), device_id_type=MESH
            )

        return 0

    lax.fori_loop(0, half, greet_source, 0)
    pl.semaphore_wait(barrier, peers + half - jnp.where(k == t // half, 1, 0))

    def send_phase(n):
        def send_block(i, _):
            tt = lax.rem(t + i // 4, tms)
            part = lax.rem(mine + 2 * half - tt % half - n, half)
            high = lax.rem(g // (2 * half) + i // 2 % 2, 2)
            gg = (high * half + part) * 2 + lax.rem(g + i, 2)
            src = s_ref.at[gg * tms + tt]
            dst = x_ref.at[k, mine, g // (2 * half) * 2 + g % 2, t]
            here = (tt == t) & (gg == g)

            @pl.when(here)
            def _():
                pltpu.make_async_copy(src, dst, recv1.at[n]).start()

            @pl.when(jnp.logical_not(here))
            def _():
                pltpu.make_async_remote_copy(
                    src_ref=src,
                    dst_ref=dst,
                    send_sem=send1,
                    recv_sem=recv1.at[n],
                    device_id=(tt, 2 * gg + k),
                    device_id_type=MESH,
                ).start()

            return 0

        lax.fori_loop(0, 4 * tms, send_block, 0)

    for n in range(LEAD):
        send_phase(n)

    wide = tms * LANES
    lane = lax.broadcasted_iota(jnp.int32, (16, LANES), 1)
    low = lane < LANES // 2
    quarter = lane % (LANES // 2) < LANES // 4
    block = ants * 4
    slot = t % half
    dims = (((1,), (1,)), ((), ()))

    def phase(n, _):
        part = lax.rem(first_part + n, half)
        arrived = x_ref.at[k, part]
        pltpu.make_async_copy(arrived, arrived, recv1.at[n]).wait()
        pltpu.make_async_remote_copy(
            src_ref=arrived,
            dst_ref=arrived,
            send_sem=send3,
            recv_sem=recv3.at[n],
            device_id=sibling,
            device_id_type=MESH,
        ).start()

        @pl.when(n + LEAD < half)
        def _():
            send_phase(n + LEAD)

        other = x_ref.at[1 - k, part]
        pltpu.make_async_copy(other, other, recv3.at[n]).wait()

        def assemble(i, _):
            high, kk = i // 4, i % 2
            base = pl.multiple_of(i % 4 * ants, ants)
            for tt in range(tms):
                right[part, high, pl.ds(base, ants), tt * LANES : (tt + 1) * LANES] = x_ref[
                    kk, part, i // 2, tt, :ants, :
                ]
            for tt in range(0, tms, 2):
                h0 = x_ref[kk, part, i // 2, tt, ants:, :].astype(jnp.float32)
                h1 = x_ref[kk, part, i // 2, tt + 1, ants:, :].astype(jnp.float32)
                top = jnp.where(low, h0, pltpu.roll(h1, LANES // 2, 1))
                bottom = jnp.where(low, pltpu.roll(h0, LANES // 2, 1), h1)
                at = wide + tt // 2 * LANES
                right[part, high, pl.ds(base, ants // 2), at : at + LANES] = top.astype(
                    jnp.bfloat16
                )
                right[part, high, pl.ds(base + ants // 2, ants // 2), at : at + LANES] = (
                    bottom.astype(jnp.bfloat16)
                )
            return 0

        lax.fori_loop(0, 8, assemble, 0)

        def swap(i, _):
            at = pl.multiple_of(i * 16, 16)
            for tile in range(right.shape[3] // LANES):
                cols = slice(tile * LANES, (tile + 1) * LANES)
                kept = right[part, k, pl.ds(at, 16), cols]
                left[part, 0, pl.ds(at, 16), cols] = kept
                v = kept.astype(jnp.float32)
                if tile < tms:
                    v = pltpu.roll(v, LANES // 2, 1)
                    v = jnp.where(low, v, -v)
                else:
                    v = jnp.where(
                        quarter, pltpu.roll(v, LANES - LANES // 4, 1), -pltpu.roll(v, LANES // 4, 1)
                    )
                left[part, 1, pl.ds(at, 16), cols] = v.astype(jnp.bfloat16)
            return 0

        lax.fori_loop(0, block // 16, swap, 0)

        def piece(row_part, col_part):
            value = lax.dot_general(
                left[row_part].reshape(2 * block, -1),
                right[col_part].reshape(2 * block, -1),
                dims,
                preferred_element_type=jnp.float32,
            )
            value = (value * scale).astype(jnp.bfloat16).reshape(2, block, 2 * block)
            target = half * k + row_part
            here = (t == target) & (k == t // half)
            for high in range(2):
                cols = pl.ds(pl.multiple_of((high * half + col_part) * block, block), block)
                outs[row_part, :, :, cols] = value[:, :, high * block : (high + 1) * block]
                src = outs.at[row_part, :, :, cols]
                dst = r_ref.at[:, slot, :, cols]

                @pl.when(here)
                def _():
                    pltpu.make_async_copy(src, dst, recv2).start()

                @pl.when(jnp.logical_not(here))
                def _():
                    pltpu.make_async_remote_copy(
                        src_ref=src,
                        dst_ref=dst,
                        send_sem=send2,
                        recv_sem=recv2,
                        device_id=(target, 2 * g + t // half),
                        device_id_type=MESH,
                    ).start()

        def new_piece(i, _):
            older = i // 2
            other = lax.rem(first_part + older, half)
            swap_roles = i % 2 == 1
            piece(jnp.where(swap_roles, part, other), jnp.where(swap_roles, other, part))
            return 0

        lax.fori_loop(0, 2 * n + 1, new_piece, 0)
        return 0

    lax.fori_loop(0, half, phase, 0)
    pltpu.make_async_copy(r_ref, r_ref, recv2).wait()

    pltpu.make_async_copy(x_ref.at[k], x_ref.at[k], send3).wait()
    sent = s_ref.at[pl.ds(0, peers - 1)]
    pltpu.make_async_copy(sent, sent, send1).wait()

    @pl.when(k == t // half)
    def _():
        kept = outs.at[pl.ds(0, half - 1)]
        pltpu.make_async_copy(kept, kept, send2).wait()

    @pl.when(k != t // half)
    def _():
        pltpu.make_async_copy(outs, outs, send2).wait()


def local(voltages, window):
    tms, freqs = lax.axis_size("tm"), lax.axis_size("freq")
    groups = freqs // 2
    half = tms // 2
    spectra = channelize(voltages, window)
    antennas, spec_here, _, channels = spectra.shape
    assert channels == tms * groups
    blocks = pack(spectra)
    rows = blocks.shape[1]
    total = antennas * freqs
    row_count = total // tms
    depth = 2 * spec_here * tms
    result = pl.pallas_call(
        functools.partial(correlate_kernel, tms, groups, (spec_here * tms) ** (-0.5)),
        out_shape=jax.ShapeDtypeStruct((2, half, row_count, total), jnp.bfloat16),
        in_specs=[pl.BlockSpec(memory_space=pltpu.VMEM)],
        out_specs=pl.BlockSpec(memory_space=pl.ANY),
        scratch_shapes=[
            pltpu.VMEM((2, half, groups // half, tms, rows, LANES), jnp.bfloat16),
            pltpu.VMEM((half, 2, row_count, depth), jnp.bfloat16),
            pltpu.VMEM((half, 2, row_count, depth), jnp.bfloat16),
            pltpu.VMEM((half, 2, row_count, total), jnp.bfloat16),
            pltpu.SemaphoreType.DMA,
            pltpu.SemaphoreType.DMA((half,)),
            pltpu.SemaphoreType.DMA,
            pltpu.SemaphoreType.DMA,
            pltpu.SemaphoreType.DMA,
            pltpu.SemaphoreType.DMA((half,)),
        ],
        compiler_params=pltpu.CompilerParams(
            collective_id=0, has_side_effects=True, vmem_limit_bytes=40 << 20
        ),
        cost_estimate=pl.CostEstimate(
            flops=2 * 2 * (total // 2) * total * depth, bytes_accessed=8 << 20, transcendentals=0
        ),
    )(blocks)
    return result.astype(jnp.float32)


def solution(mesh):
    return jax.shard_map(
        local,
        mesh=mesh,
        in_specs=(P("freq", "tm"), P()),
        out_specs=P(None, "freq", "tm", None),
        check_vma=False,
    )
```

time: 105 us -> 91.8 us (0.87)
  the two profiles are of different devices: /device:TPU:26 before, /device:TPU:24 now
where the time goes in v2:
time: 91.8 us; the launch traced here: 91.7 us
  Pallas kernels  72.8 us (79%)
  matrix products  5.31 us (6%)
  other arithmetic  3.55 us (4%)
  waiting for transfers between devices  3.47 us (4%)
  local copies, waits for them, and re-layouts  3.42 us (4%)
  starting transfers between devices  3.06 us (3%)
    pallas_call x1, Pallas kernels, local(): pl.pallas_call(functools.partial(correlate_kernel, tms, groups, (spec_her...  72.8 us
    dot_general x1, matrix products, channelize(): jnp.dot(filtered.reshape(-1, period), dft_table(period, channels), precis...  5.31 us
    ppermute x1, waiting for transfers between devices, from_behind(): lax.ppermute(value, axis, [(source, source + steps) for source in range(f...  3.47 us
    ppermute x1, starting transfers between devices, from_behind(): lax.ppermute(value, axis, [(source, source + steps) for source in range(f...  3.06 us
    convert_element_type x1, other arithmetic, local(): return result.astype(jnp.float32)  2.48 us
  transfers between devices with their start and end apart: 1, of which 1 were waited for; matrix products, arithmetic and copies ran while one was open for 1% of the time, Pallas kernels for 0%

profile of v2, /device:TPU:24, one launch (start us, length us, event | category | flops | bytes accessed | tf_op | source)
XLA Modules:
  0.0 91.7 jit_solution(13101225807797239493)
XLA Ops:
  0.0 0.0 copy-start
  0.0 1.8 %copy.9 = bf16[4,8,96,256]{3,2,1,0:T(8,128)(2,1)S(1)} copy(bf16[4,8,96,256]{3,1,2,0:T(8,128)(2,1)} %bitcast.35) | data formatting | bytes 3145728
  1.8 3.1 %collective-permute-start = (bf16[32,7,256]{2,1,0:T(8,128)(2,1)S(1)}, bf16[32,7,256]{2,1,0:T(8,128)(2,1)S(1)}, u32[]{:S(2)}, u32[]{:S(2)}) collective-permute-start(bf16[32,7,256]{2,1,0:T(8,128)(2,1)S(1)} %slice.76), channel_id=1, source_target_pairs={{0,32},{32,64},{64,96},{96,128},{128,160},{160,192},{192,224},{1,3... | collective-permute-start | bytes 344072 | tf_op jit(solution)/shard_map/ppermute | solution.py:19
  4.9 0.5 sine_negate_fusion
  5.4 0.0 copy-done
  5.5 3.5 %collective-permute-done = bf16[32,7,256]{2,1,0:T(8,128)(2,1)S(1)} collective-permute-done((bf16[32,7,256]{2,1,0:T(8,128)(2,1)S(1)}, bf16[32,7,256]{2,1,0:T(8,128)(2,1)S(1)}, u32[]{:S(2)}, u32[]{:S(2)}) %collective-permute-start) | collective-permute-done | bytes 114720 | tf_op jit(solution)/shard_map/ppermute | solution.py:19
  9.0 0.4 maximum_convert_fusion
  9.4 5.3 %fusion.16 = bf16[32,96,2,128]{3,1,2,0:T(8,128)(2,1)S(1)} fusion(f32[2,128,256,1]{2,1,0,3:T(8,128)S(1)} %bitcast.36, f32[32,103,256]{2,1,0:T(8,128)S(1)} %maximum_convert_fusion, f32[256]{0:T(256)S(1)} %bitcast.43, f32[256]{0:T(256)S(1)} %bitcast.44, f32[256]{0:T(256)S(1)} %bitcast.38, f32[256]{0:T(256)S(1)} %bitcast.39, f32[256]{0:T(256)S(1)} %bitcast.40, ...), kind=kOutput, calls=%fused_computation.18 | convolution fusion | flops 2428502016 | bytes 27009024 | tf_op jit(solution)/shard_map/dot_general | solution.py:40
  14.7 0.1 slice.85
  14.9 1.0 %copy.6 = bf16[128,32,128]{2,1,0:T(8,128)(2,1)S(1)} copy(bf16[128,32,128]{0,2,1:T(8,128)(2,1)S(1)} %bitcast.32) | data formatting | bytes 2097152 | tf_op jit(solution)/shard_map/reshape | solution.py:49
  15.9 0.4 copy.7
  16.3 0.1 pad_maximum_fusion.s_ref
  16.4 72.8 %shard_map.28 = bf16[2,4,128,1024]{3,2,1,0:T(8,128)(2,1)S(1)} custom-call(bf16[128,48,128]{2,1,0:T(8,128)(2,1)S(1)} %pad_maximum_fusion.s_ref), custom_call_target="tpu_custom_call" | custom-call | flops 3221225472 | bytes 8388608 | tf_op jit(solution)/shard_map/pallas_call | solution.py:264
  89.2 2.5 %convert_element_type.17 = f32[2,4,128,1024]{3,2,1,0:T(8,128)} convert(bf16[2,4,128,1024]{3,2,1,0:T(8,128)(2,1)S(1)} %shard_map.28) | non-fusion elementwise | flops 1048576 | bytes 6291456 | tf_op jit(solution)/shard_map/convert_element_type | solution.py:288
  (5 shorter events, 0.1 us)
Async XLA Ops:
  0.0 5.4 %copy-start = (f32[8,256]{1,0:T(8,128)S(1)}, f32[8,256]{1,0:T(8,128)}, u32[]{:S(2)}) copy-start(f32[8,256]{1,0:T(8,128)} %param.3) | copy-start | bytes 24580
  1.8 7.1 %collective-permute-start = (bf16[32,7,256]{2,1,0:T(8,128)(2,1)S(1)}, bf16[32,7,256]{2,1,0:T(8,128)(2,1)S(1)}, u32[]{:S(2)}, u32[]{:S(2)}) collective-permute-start(bf16[32,7,256]{2,1,0:T(8,128)(2,1)S(1)} %slice.76), channel_id=1, source_target_pairs={{0,32},{32,64},{64,96},{96,128},{128,160},{160,192},{192,224},{1,3... | collective-permute-start | bytes 344072 | tf_op jit(solution)/shard_map/ppermute | solution.py:19

commit v3 on v2

--- a/solution.py
+++ b/solution.py
@@ -3,6 +3,7 @@
 
 import jax
 import jax.numpy as jnp
+import numpy as np
 from jax import lax
 from jax.experimental import pallas as pl
 from jax.experimental.pallas import tpu as pltpu
@@ -13,47 +14,185 @@
 LEAD = 4
 
 
-def from_behind(value, axis, steps):
-    count = lax.axis_size(axis)
-    first, last = (max(0, -steps), min(count, count - steps))
-    return lax.ppermute(value, axis, [(source, source + steps) for source in range(first, last)])
-
-
 def dft_table(length, channels):
-    sample = jnp.arange(length, dtype=jnp.int32)[:, None]
-    channel = jnp.arange(channels, dtype=jnp.int32)[None, :]
-    phase = (sample * channel % length).astype(jnp.float32) * (2.0 * math.pi / length)
-    return jnp.concatenate([jnp.cos(phase), -jnp.sin(phase)], axis=1) * length ** (-0.5)
-
-
-def channelize(voltages, window):
-    taps, period = window.shape
+    sample, channel = np.arange(length), np.arange(channels)
+    phase = (channel[:, None] * sample[None, :] % length) * (2.0 * math.pi / length)
+    rows = np.concatenate([np.cos(phase), -np.sin(phase)], axis=0) * length ** (-0.5)
+    high = rows.astype(jnp.bfloat16)
+    low = (rows - high.astype(np.float64)).astype(jnp.bfloat16)
+    return np.concatenate([high, low], axis=0)
+
+
+def polyphase(frames, w_ref, tile, first, groups, taps, store):
+    cols = slice(tile * LANES, (tile + 1) * LANES)
+    weights = [w_ref[k : k + 1, cols] for k in range(taps)]
+
+    def group(i, held):
+        held = list(held)
+        for u in range(8):
+            at = first + i * 8 + u
+            held.append(frames(at + taps - 1, tile))
+            value = weights[0] * held[0]
+            for k in range(1, taps):
+                value = value + weights[k] * held[k]
+            held.pop(0)
+            store(at, tile, value)
+        return tuple(held)
+
+    lax.fori_loop(0, groups, group, tuple(frames(first + j, tile) for j in range(taps - 1)))
+
+
+def channelize(
+    v_ref, w_ref, c_ref, s_ref, joined, early, late, turned, load_sem, halo_sems, t, f, tms, before
+):
+    taps, period = w_ref.shape
+    antennas, samples = v_ref.shape
+    spec = samples // period
+    first, main = spec // 3, 2 * spec // 3
+    tiles = period // LANES
     channels = period // 2
-    antennas = voltages.shape[0]
-    blocks = voltages.reshape(antennas, -1, period)
-    spec_here = blocks.shape[1]
-    history = from_behind(blocks[:, spec_here - (taps - 1) :, :], "tm", 1)
-    joined = jnp.concatenate([history, blocks], axis=1).astype(jnp.float32)
-    filtered = jnp.zeros((antennas, spec_here, period), jnp.float32)
-    for k in range(taps):
-        filtered = filtered + window[k][None, None, :] * joined[:, k : k + spec_here, :]
-    spectra = jnp.dot(
-        filtered.reshape(-1, period), dft_table(period, channels), precision=lax.Precision.HIGHEST
-    )
-    return spectra.reshape(antennas, spec_here, 2, channels).astype(jnp.bfloat16)
-
-
-def pack(spectra):
-    antennas, spec, _, channels = spectra.shape
-    main = 2 * spec // 3
-    first = spectra[:, :main].transpose(3, 0, 2, 1).reshape(channels, antennas, LANES)
-    rest = spectra[:, main:].reshape(2, antennas // 2, spec - main, 2, channels)
-    rest = rest.transpose(4, 1, 0, 3, 2).reshape(channels, antennas // 2, LANES)
-    return jnp.concatenate([first, rest], axis=1)
+    halo = (taps - 1) * period
+    paired = antennas // 2
+    eighth = antennas // 4
+    main_stride, rest_stride = main + 1, first + 1
+    turn_stride = s_ref.shape[1] + 1
+
+    def frames(j, tile):
+        at = pl.multiple_of(j * period + tile * LANES, LANES)
+        return joined[:, pl.ds(at, LANES)].astype(jnp.float32)
+
+    def store_main(at, tile, value):
+        for h in range(2):
+            rows = pl.ds(h * paired * main_stride + at - first, paired, stride=main_stride)
+            late[tile, rows, :] = value[h * paired : (h + 1) * paired]
+
+    def store_rest(at, tile, value):
+        for h in range(4):
+            rows = pl.ds(h * eighth * rest_stride + at, eighth, stride=rest_stride)
+            early[tile, rows, :] = value[h * eighth : (h + 1) * eighth]
+
+    @pl.when(t == 0)
+    def _():
+        joined[:, :halo] = jnp.zeros((antennas, halo), jnp.bfloat16)
+
+    own = joined.at[:, pl.ds(halo, samples)]
+    pltpu.make_async_copy(v_ref, own, load_sem).wait()
+    for tile in range(tiles):
+        polyphase(frames, w_ref, tile, first, main // 8, taps, store_main)
+    for tile in range(tiles):
+        polyphase(frames, w_ref, tile, 8, first // 8 - 1, taps, store_rest)
+
+    before()
+    last = joined.at[:, pl.ds(samples, halo)]
+    landing = joined.at[:, pl.ds(0, halo)]
+
+    @pl.when(t < tms - 1)
+    def _():
+        pltpu.make_async_remote_copy(
+            src_ref=last,
+            dst_ref=landing,
+            send_sem=halo_sems.at[0],
+            recv_sem=halo_sems.at[1],
+            device_id=(lax.rem(t + 1, tms), f),
+            device_id_type=MESH,
+        ).start()
+
+    lane = lax.broadcasted_iota(jnp.int32, (channels, LANES), 1)
+    low = lane < LANES // 2
+    quarter = lane % (LANES // 2) < LANES // 4
+    dims = (((1,), (1,)), ((), ()))
+
+    def dft(x):
+        high = x.astype(jnp.bfloat16)
+        rest = (x - high.astype(jnp.float32)).astype(jnp.bfloat16)
+        y = lax.dot_general(c_ref[...], high, dims, preferred_element_type=jnp.float32)
+        z = lax.dot_general(
+            c_ref[: 2 * channels, :], rest, dims, preferred_element_type=jnp.float32
+        )
+        return y[: 2 * channels] + y[2 * channels :] + z
+
+    def gather(ref, starts, count):
+        return jnp.concatenate(
+            [
+                jnp.concatenate([ref[tile, pl.ds(at, count), :] for at in starts], axis=0)
+                for tile in range(tiles)
+            ],
+            axis=1,
+        )
+
+    def turn(row, value):
+        turned[pl.ds(row, channels, stride=turn_stride), :] = value
+
+    def main_part(i, _):
+        starts = [(h * paired + i * 2 + p) * main_stride for p in range(2) for h in range(2)]
+        y = dft(gather(late, starts, main))
+        for p in range(2):
+            cols = slice(p * LANES, (p + 1) * LANES)
+            re, im = y[:channels, cols], y[channels:, cols]
+            turn(i * 2 + p, jnp.where(low, re, pltpu.roll(im, LANES // 2, 1)))
+            turn(i * 2 + p + paired, jnp.where(low, pltpu.roll(re, LANES // 2, 1), im))
+        return 0
+
+    lax.fori_loop(0, paired // 2, main_part, 0, unroll=4)
+
+    @pl.when(t > 0)
+    def _():
+        pltpu.make_async_copy(landing, landing, halo_sems.at[1]).wait()
+
+    for tile in range(tiles):
+        polyphase(frames, w_ref, tile, 0, 1, taps, store_rest)
+
+    def rest_part(i, _):
+        starts = [(h * eighth + i * 2 + p) * rest_stride for p in range(2) for h in range(4)]
+        y = dft(gather(early, starts, first))
+        for p in range(2):
+            cols = slice(p * LANES, (p + 1) * LANES)
+            re, im = y[:channels, cols], y[channels:, cols]
+            row = antennas + i * 2 + p
+            turn(row, jnp.where(quarter, re, pltpu.roll(im, LANES // 4, 1)))
+            turn(row + eighth, jnp.where(quarter, pltpu.roll(re, LANES - LANES // 4, 1), im))
+        return 0
+
+    lax.fori_loop(0, eighth // 2, rest_part, 0, unroll=4)
+
+    def pack(i, _):
+        for u in range(16):
+            c = i * 16 + u
+            s_ref[c] = turned[pl.ds(c * turn_stride, s_ref.shape[1]), :].astype(jnp.bfloat16)
+        return 0
+
+    lax.fori_loop(0, channels // 16, pack, 0)
+
+    @pl.when(t < tms - 1)
+    def _():
+        pltpu.make_async_copy(last, last, halo_sems.at[0]).wait()
 
 
 def correlate_kernel(
-    tms, groups, scale, s_ref, r_ref, x_ref, right, left, outs, send1, recv1, send2, recv2, send3, recv3
+    tms,
+    groups,
+    scale,
+    v_ref,
+    w_ref,
+    c_ref,
+    r_ref,
+    joined,
+    early,
+    late,
+    turned,
+    s_ref,
+    x_ref,
+    right,
+    left,
+    outs,
+    load_sem,
+    halo_sems,
+    send1,
+    recv1,
+    send2,
+    recv2,
+    send3,
+    recv3,
 ):
     t, f = lax.axis_index("tm"), lax.axis_index("freq")
     g, k = f // 2, f % 2
@@ -65,6 +204,10 @@
     mine = g // 2 % half
     first_part = lax.rem(mine + t, half)
 
+    halo = joined.shape[1] - v_ref.shape[1]
+    pltpu.make_async_copy(
+        v_ref, joined.at[:, pl.ds(halo, v_ref.shape[1])], load_sem
+    ).start()
     barrier = pltpu.get_barrier_semaphore()
 
     def greet(i, _):
@@ -87,7 +230,26 @@
         return 0
 
     lax.fori_loop(0, half, greet_source, 0)
-    pl.semaphore_wait(barrier, peers + half - jnp.where(k == t // half, 1, 0))
+
+    def await_greetings():
+        pl.semaphore_wait(barrier, peers + half - jnp.where(k == t // half, 1, 0))
+
+    channelize(
+        v_ref,
+        w_ref,
+        c_ref,
+        s_ref,
+        joined,
+        early,
+        late,
+        turned,
+        load_sem,
+        halo_sems,
+        t,
+        f,
+        tms,
+        await_greetings,
+    )
 
     def send_phase(n):
         def send_block(i, _):
@@ -253,24 +415,33 @@
     tms, freqs = lax.axis_size("tm"), lax.axis_size("freq")
     groups = freqs // 2
     half = tms // 2
-    spectra = channelize(voltages, window)
-    antennas, spec_here, _, channels = spectra.shape
+    taps, period = window.shape
+    antennas, samples = voltages.shape
+    spec_here = samples // period
+    channels = period // 2
     assert channels == tms * groups
-    blocks = pack(spectra)
-    rows = blocks.shape[1]
+    rows = antennas * 3 // 2
     total = antennas * freqs
     row_count = total // tms
     depth = 2 * spec_here * tms
+    vmem = pl.BlockSpec(memory_space=pltpu.VMEM)
     result = pl.pallas_call(
         functools.partial(correlate_kernel, tms, groups, (spec_here * tms) ** (-0.5)),
         out_shape=jax.ShapeDtypeStruct((2, half, row_count, total), jnp.bfloat16),
-        in_specs=[pl.BlockSpec(memory_space=pltpu.VMEM)],
+        in_specs=[pl.BlockSpec(memory_space=pl.ANY), vmem, vmem],
         out_specs=pl.BlockSpec(memory_space=pl.ANY),
         scratch_shapes=[
+            pltpu.VMEM((antennas, samples + (taps - 1) * period), jnp.bfloat16),
+            pltpu.VMEM((period // LANES, antennas * (spec_here // 3 + 1), LANES), jnp.float32),
+            pltpu.VMEM((period // LANES, antennas * (2 * spec_here // 3 + 1), LANES), jnp.float32),
+            pltpu.VMEM((channels * (rows + 1), LANES), jnp.float32),
+            pltpu.VMEM((channels, rows, LANES), jnp.bfloat16),
             pltpu.VMEM((2, half, groups // half, tms, rows, LANES), jnp.bfloat16),
             pltpu.VMEM((half, 2, row_count, depth), jnp.bfloat16),
             pltpu.VMEM((half, 2, row_count, depth), jnp.bfloat16),
             pltpu.VMEM((half, 2, row_count, total), jnp.bfloat16),
+            pltpu.SemaphoreType.DMA,
+            pltpu.SemaphoreType.DMA((2,)),
             pltpu.SemaphoreType.DMA,
             pltpu.SemaphoreType.DMA((half,)),
             pltpu.SemaphoreType.DMA,
@@ -279,12 +450,12 @@
             pltpu.SemaphoreType.DMA((half,)),
         ],
         compiler_params=pltpu.CompilerParams(
-            collective_id=0, has_side_effects=True, vmem_limit_bytes=40 << 20
+            collective_id=0, has_side_effects=True, vmem_limit_bytes=48 << 20
         ),
         cost_estimate=pl.CostEstimate(
             flops=2 * 2 * (total // 2) * total * depth, bytes_accessed=8 << 20, transcendentals=0
         ),
-    )(blocks)
+    )(voltages, window, jnp.asarray(dft_table(period, channels)))
     return result.astype(jnp.float32)
 
 

time: 91.8 us -> 83.4 us (0.908); the launches traced: 91.7 us -> 82.1 us
  matrix products: 5.31 us -> 0 us
  Pallas kernels: 72.8 us -> 76.5 us
  waiting for transfers between devices: 3.47 us -> 0 us
  starting transfers between devices: 3.06 us -> 0 us
  other arithmetic: 3.55 us -> 2.48 us
    dot_general x1 -> x0, matrix products: 5.31 us -> none  [channelize(): jnp.dot(filtered.reshape(-1, period), dft_table(period, channels), precis...]
    pallas_call x1, Pallas kernels: 72.8 us -> 76.5 us  [local(): pl.pallas_call(functools.partial(correlate_kernel, tms, groups, (spec_her...]
    ppermute x1 -> x0, waiting for transfers between devices: 3.47 us -> none  [from_behind(): lax.ppermute(value, axis, [(source, source + steps) for source in range(f...]
    ppermute x1 -> x0, starting transfers between devices: 3.06 us -> none  [from_behind(): lax.ppermute(value, axis, [(source, source + steps) for source in range(f...]
    reshape x3 -> x0, local copies, waits for them, and re-layouts: 1.44 us -> none  [the longest x1 0.98 us: pack(): spectra[:, :main].transpose(3, 0, 2, 1).reshape(channels, antennas, LANES)]
    unnamed x3 -> x6, local copies, waits for them, and re-layouts: 1.78 us -> 3.05 us
  transfers between devices with their start and end apart: 1 -> 0, of which waited for: 1 -> 0; matrix products, arithmetic and copies ran while one was open for 1% -> 0% of each run, Pallas kernels for 0% -> 0%
where the time goes in v3:
time: 83.4 us; the launch traced here: 82.1 us
  Pallas kernels  76.5 us (92%)
  local copies, waits for them, and re-layouts  3.05 us (4%)
  other arithmetic  2.48 us (3%)
    pallas_call x1, Pallas kernels, local(): pl.pallas_call(functools.partial(correlate_kernel, tms, groups, (spec_her...  76.5 us
    unnamed x6, local copies, waits for them, and re-layouts  3.05 us
    convert_element_type x1, other arithmetic, local(): return result.astype(jnp.float32)  2.48 us

profile of v3, /device:TPU:24, one launch (start us, length us, event | category | flops | bytes accessed | tf_op | source)
XLA Modules:
  0.0 82.1 jit_solution(6354062997441088719)
XLA Ops:
  0.0 0.0 copy-start
  0.0 1.4 %copy-done = bf16[32,24576]{1,0:T(8,128)(2,1)S(1)} copy-done((bf16[32,24576]{1,0:T(8,128)(2,1)S(1)}, bf16[32,24576]{1,0:T(8,128)(2,1)}, u32[]{:S(2)}) %copy-start) | copy-done | bytes 1572888
  1.4 0.0 copy-start.1
  1.4 0.7 copy-done.1
  2.1 0.0 copy-start.2
  2.1 0.9 %copy-done.2 = bf16[512,256]{1,0:T(8,128)(2,1)S(1)} copy-done((bf16[512,256]{1,0:T(8,128)(2,1)S(1)}, bf16[512,256]{1,0:T(8,128)(2,1)}, u32[]{:S(2)}) %copy-start.2) | copy-done | bytes 262168
  3.1 76.5 %shard_map.37 = bf16[2,4,128,1024]{3,2,1,0:T(8,128)(2,1)S(1)} custom-call(bf16[32,24576]{1,0:T(8,128)(2,1)S(1)} %copy-done, f32[8,256]{1,0:T(8,128)S(1)} %copy-done.1, bf16[512,256]{1,0:T(8,128)(2,1)S(1)} %copy-done.2), custom_call_target="tpu_custom_call" | custom-call | flops 3221225472 | bytes 8388608 | tf_op jit(solution)/shard_map/pallas_call | solution.py:428
  79.6 2.5 %convert_element_type.3 = f32[2,4,128,1024]{3,2,1,0:T(8,128)} convert(bf16[2,4,128,1024]{3,2,1,0:T(8,128)(2,1)S(1)} %shard_map.37) | non-fusion elementwise | flops 1048576 | bytes 6291456 | tf_op jit(solution)/shard_map/convert_element_type | solution.py:459
Async XLA Ops:
  0.0 1.4 %copy-start = (bf16[32,24576]{1,0:T(8,128)(2,1)S(1)}, bf16[32,24576]{1,0:T(8,128)(2,1)}, u32[]{:S(2)}) copy-start(bf16[32,24576]{1,0:T(8,128)(2,1)} %v_ref.1) | copy-start | bytes 4718596
  1.4 0.7 copy-start.1
  2.1 0.9 %copy-start.2 = (bf16[512,256]{1,0:T(8,128)(2,1)S(1)}, bf16[512,256]{1,0:T(8,128)(2,1)}, u32[]{:S(2)}) copy-start(bf16[512,256]{1,0:T(8,128)(2,1)} %constant.2.clone.c_ref) | copy-start | bytes 786436

commit v4 on v3

v4 whole, which is shorter than its diff:
```python
import functools
import math

import jax
import jax.numpy as jnp
import numpy as np
from jax import lax
from jax.experimental import pallas as pl
from jax.experimental.pallas import tpu as pltpu
from jax.sharding import PartitionSpec as P

MESH = pl.DeviceIdType.MESH
LANES = 128
EARLY = 2


def dft_table(length, channels):
    sample, channel = np.arange(length), np.arange(channels)
    phase = (channel[:, None] * sample[None, :] % length) * (2.0 * math.pi / length)
    rows = np.concatenate([np.cos(phase), -np.sin(phase)], axis=0) * length ** (-0.5)
    high = rows.astype(jnp.bfloat16)
    low = (rows - high.astype(np.float64)).astype(jnp.bfloat16)
    return np.concatenate([high, low], axis=0)


def polyphase(frames, w_ref, tile, first, groups, taps, store, beside=None):
    cols = slice(tile * LANES, (tile + 1) * LANES)
    weights = [w_ref[k : k + 1, cols] for k in range(taps)]

    def group(i, held):
        held = list(held)
        if beside is not None:
            beside(tile * groups + i)
        for u in range(8):
            at = first + i * 8 + u
            held.append(frames(at + taps - 1, tile))
            value = weights[0] * held[0]
            for k in range(1, taps):
                value = value + weights[k] * held[k]
            held.pop(0)
            store(at, tile, value)
        return tuple(held)

    lax.fori_loop(0, groups, group, tuple(frames(first + j, tile) for j in range(taps - 1)))


def channelize(
    v_ref, w_ref, c_ref, s_ref, joined, early, late, turned, loads, halo_sems, t, f, tms, greet, greetings,
    before, between,
):
    taps, period = w_ref.shape
    antennas, samples = v_ref.shape
    spec = samples // period
    first, main = spec // 3, 2 * spec // 3
    tiles = period // LANES
    channels = period // 2
    halo = (taps - 1) * period
    paired = antennas // 2
    eighth = antennas // 4
    main_stride, rest_stride = main + 1, first + 1
    turn_stride = s_ref.shape[1] + 1

    def frames(j, tile):
        at = pl.multiple_of(j * period + tile * LANES, LANES)
        return joined[:, pl.ds(at, LANES)].astype(jnp.float32)

    def store_main(at, tile, value):
        for h in range(2):
            rows = pl.ds(h * paired * main_stride + at - first, paired, stride=main_stride)
            late[tile, rows, :] = value[h * paired : (h + 1) * paired]

    def store_rest(at, tile, value):
        for h in range(4):
            rows = pl.ds(h * eighth * rest_stride + at, eighth, stride=rest_stride)
            early[tile, rows, :] = value[h * eighth : (h + 1) * eighth]

    @pl.when(t == 0)
    def _():
        joined[:, :halo] = jnp.zeros((antennas, halo), jnp.bfloat16)

    steps = tiles * main // 8
    each = greetings // 2 // steps
    lax.fori_loop(0, greetings - each * steps, lambda i, _: greet(i), 0)
    for load in loads:
        load.wait()
    for tile in range(tiles):
        polyphase(
            frames,
            w_ref,
            tile,
            first,
            main // 8,
            taps,
            store_main,
            lambda i: [greet(greetings - 1 - i * each - u) for u in range(each)],
        )

    lane = lax.broadcasted_iota(jnp.int32, (channels, LANES), 1)
    low = lane < LANES // 2
    quarter = lane % (LANES // 2) < LANES // 4
    dims = (((1,), (1,)), ((), ()))

    def dft(x):
        high = x.astype(jnp.bfloat16)
        rest = (x - high.astype(jnp.float32)).astype(jnp.bfloat16)
        y = lax.dot_general(c_ref[...], high, dims, preferred_element_type=jnp.float32)
        z = lax.dot_general(
            c_ref[: 2 * channels, :], rest, dims, preferred_element_type=jnp.float32
        )
        return y[: 2 * channels] + y[2 * channels :] + z

    def gather(ref, starts, count):
        return jnp.concatenate(
            [
                jnp.concatenate([ref[tile, pl.ds(at, count), :] for at in starts], axis=0)
                for tile in range(tiles)
            ],
            axis=1,
        )

    def turn(row, value):
        turned[pl.ds(row, channels, stride=turn_stride), :] = value

    def pack(at, count):
        def some(i, _):
            for u in range(16):
                c = i * 16 + u
                s_ref[c, pl.ds(at, count), :] = turned[
                    pl.ds(c * turn_stride + at, count), :
                ].astype(jnp.bfloat16)
            return 0

        lax.fori_loop(0, channels // 16, some, 0)

    def main_part(i, _):
        starts = [(h * paired + i * 2 + p) * main_stride for p in range(2) for h in range(2)]
        y = dft(gather(late, starts, main))
        for p in range(2):
            cols = slice(p * LANES, (p + 1) * LANES)
            re, im = y[:channels, cols], y[channels:, cols]
            turn(i * 2 + p, jnp.where(low, re, pltpu.roll(im, LANES // 2, 1)))
            turn(i * 2 + p + paired, jnp.where(low, pltpu.roll(re, LANES // 2, 1), im))
        return 0

    lax.fori_loop(0, paired // 2, main_part, 0, unroll=4)
    pack(0, antennas)
    for tile in range(tiles):
        polyphase(frames, w_ref, tile, 8, first // 8 - 1, taps, store_rest)

    before()
    last = joined.at[:, pl.ds(samples, halo)]
    landing = joined.at[:, pl.ds(0, halo)]

    @pl.when(t < tms - 1)
    def _():
        pltpu.make_async_remote_copy(
            src_ref=last,
            dst_ref=landing,
            send_sem=halo_sems.at[0],
            recv_sem=halo_sems.at[1],
            device_id=(lax.rem(t + 1, tms), f),
            device_id_type=MESH,
        ).start()

    between()

    @pl.when(t > 0)
    def _():
        pltpu.make_async_copy(landing, landing, halo_sems.at[1]).wait()

    for tile in range(tiles):
        polyphase(frames, w_ref, tile, 0, 1, taps, store_rest)

    def rest_part(i, _):
        starts = [(h * eighth + i * 2 + p) * rest_stride for p in range(2) for h in range(4)]
        y = dft(gather(early, starts, first))
        for p in range(2):
            cols = slice(p * LANES, (p + 1) * LANES)
            re, im = y[:channels, cols], y[channels:, cols]
            row = antennas + i * 2 + p
            turn(row, jnp.where(quarter, re, pltpu.roll(im, LANES // 4, 1)))
            turn(row + eighth, jnp.where(quarter, pltpu.roll(re, LANES - LANES // 4, 1), im))
        return 0

    lax.fori_loop(0, eighth // 2, rest_part, 0, unroll=4)
    pack(antennas, paired)

    @pl.when(t < tms - 1)
    def _():
        pltpu.make_async_copy(last, last, halo_sems.at[0]).wait()


def correlate_kernel(
    tms,
    groups,
    scale,
    v_ref,
    window_ref,
    table_ref,
    r_ref,
    joined,
    w_ref,
    c_ref,
    early,
    late,
    turned,
    s_ref,
    x_ref,
    right,
    left,
    outs,
    load_sems,
    halo_sems,
    send1,
    recv1,
    send2,
    recv2,
    send3,
    recv3,
):
    t, f = lax.axis_index("tm"), lax.axis_index("freq")
    g, k = f // 2, f % 2
    half = tms // 2
    peers = tms * groups
    rows = s_ref.shape[1]
    ants = 2 * rows // 3
    sibling = (t, 2 * g + 1 - k)
    mine = g // 2 % half
    my_high = g // (2 * half)

    halo = joined.shape[1] - v_ref.shape[1]
    loads = [
        pltpu.make_async_copy(source, target, load_sems.at[i])
        for i, (source, target) in enumerate(
            (
                (v_ref, joined.at[:, pl.ds(halo, v_ref.shape[1])]),
                (window_ref, w_ref),
                (table_ref, c_ref),
            )
        )
    ]
    for load in loads:
        load.start()
    barrier = pltpu.get_barrier_semaphore()

    def greet(n):
        tt, gg = lax.rem(t + n // groups, tms), lax.rem(g + n % groups, groups)
        to = jnp.where(n == 0, 2 * g + 1 - k, 2 * gg + k)
        pl.semaphore_signal(barrier, inc=1, device_id=(tt, to), device_id_type=MESH)
        return 0

    for j in range(half):
        pl.semaphore_signal(
            barrier, inc=1, device_id=(half * k + j, 2 * g + 1 - k), device_id_type=MESH
        )

    def await_greetings():
        pl.semaphore_wait(barrier, peers + jnp.where(k == t // half, 0, tms))

    def send_phase(n, first_row, row_count):
        def send_block(i, _):
            tt = lax.rem(t + i // 2, tms)
            part = lax.rem(mine + 2 * half - tt % half - n // 2, half)
            high = lax.rem(my_high + tt // half + n % 2, 2)
            gg = (high * half + part) * 2 + lax.rem(g + i, 2)
            some = pl.ds(first_row, row_count)
            src = s_ref.at[gg * tms + tt, some]
            dst = x_ref.at[k, mine, my_high, g % 2, t, some]
            here = (tt == t) & (gg == g)

            @pl.when(here)
            def _():
                pltpu.make_async_copy(src, dst, recv1.at[n]).start()

            @pl.when(jnp.logical_not(here))
            def _():
                pltpu.make_async_remote_copy(
                    src_ref=src,
                    dst_ref=dst,
                    send_sem=send1,
                    recv_sem=recv1.at[n],
                    device_id=(tt, 2 * gg + k),
                    device_id_type=MESH,
                ).start()

            return 0

        lax.fori_loop(0, 2 * tms, send_block, 0)
        return 0

    def send_phases(first, last, first_row, row_count):
        lax.fori_loop(first, last, lambda n, _: send_phase(n, first_row, row_count), 0)

    channelize(
        v_ref,
        w_ref,
        c_ref,
        s_ref,
        joined,
        early,
        late,
        turned,
        loads,
        halo_sems,
        t,
        f,
        tms,
        greet,
        peers,
        await_greetings,
        lambda: send_phases(0, EARLY, 0, ants),
    )
    send_phases(0, EARLY, ants, rows - ants)
    send_phases(EARLY, tms, 0, rows)

    wide = tms * LANES
    lane = lax.broadcasted_iota(jnp.int32, (16, LANES), 1)
    low = lane < LANES // 2
    quarter = lane % (LANES // 2) < LANES // 4
    block = ants * 4
    own = block // 2
    slot = t % half
    dims = (((1,), (1,)), ((), ()))

    def place(n):
        return lax.rem(my_high + t // half + n % 2, 2), lax.rem(mine + t + n // 2, half)

    def phase(n, _):
        high, part = place(n)
        arrived = x_ref.at[k, part, high]
        pltpu.make_async_copy(arrived, arrived, recv1.at[n]).wait()
        pltpu.make_async_remote_copy(
            src_ref=arrived,
            dst_ref=arrived,
            send_sem=send3,
            recv_sem=recv3.at[n],
            device_id=sibling,
            device_id_type=MESH,
        ).start()
        other = x_ref.at[1 - k, part, high]
        pltpu.make_async_copy(other, other, recv3.at[n]).wait()

        def assemble(i, _):
            kk, low_g = i % 2, i // 2
            base = pl.multiple_of(i * ants, ants)
            for tt in range(tms):
                right[n, pl.ds(base, ants), tt * LANES : (tt + 1) * LANES] = x_ref[
                    kk, part, high, low_g, tt, :ants, :
                ]
            for tt in range(0, tms, 2):
                h0 = x_ref[kk, part, high, low_g, tt, ants:, :].astype(jnp.float32)
                h1 = x_ref[kk, part, high, low_g, tt + 1, ants:, :].astype(jnp.float32)
                top = jnp.where(low, h0, pltpu.roll(h1, LANES // 2, 1))
                bottom = jnp.where(low, pltpu.roll(h0, LANES // 2, 1), h1)
                cols = slice(wide + tt // 2 * LANES, wide + (tt // 2 + 1) * LANES)
                right[n, pl.ds(base, ants // 2), cols] = top.astype(jnp.bfloat16)
                right[n, pl.ds(base + ants // 2, ants // 2), cols] = bottom.astype(jnp.bfloat16)
            return 0

        lax.fori_loop(0, 4, assemble, 0)

        def swap(i, _):
            at = pl.multiple_of(i * 16, 16)
            for tile in range(right.shape[2] // LANES):
                cols = slice(tile * LANES, (tile + 1) * LANES)
                kept = right[n, pl.ds(pl.multiple_of(k * own + at, 16), 16), cols]
                left[n, 0, pl.ds(at, 16), cols] = kept
                v = kept.astype(jnp.float32)
                if tile < tms:
                    v = pltpu.roll(v, LANES // 2, 1)
                    v = jnp.where(low, v, -v)
                else:
                    v = jnp.where(
                        quarter, pltpu.roll(v, LANES - LANES // 4, 1), -pltpu.roll(v, LANES // 4, 1)
                    )
                left[n, 1, pl.ds(at, 16), cols] = v.astype(jnp.bfloat16)
            return 0

        lax.fori_loop(0, own // 16, swap, 0)

        def piece(row, row_count, col, col_count):
            value = lax.dot_general(
                left[pl.ds(row, row_count)].reshape(row_count * block, -1),
                right[pl.ds(col, col_count)].reshape(col_count * block, -1),
                dims,
                preferred_element_type=jnp.float32,
            )
            value = (value * scale).astype(jnp.bfloat16)
            value = value.reshape(row_count, 2, own, col_count * block)
            for r in range(row_count):
                to_high, to_part = place(row + r)
                target = to_high * half + to_part
                here = (t == target) & (k == t // half)
                for c in range(col_count):
                    at_high, at_part = place(col + c)
                    cols = pl.ds(pl.multiple_of((at_high * half + at_part) * block, block), block)
                    outs[row + r, :, :, cols] = value[r, :, :, c * block : (c + 1) * block]
                    src = outs.at[row + r, :, :, cols]
                    dst = r_ref.at[:, slot, pl.ds(pl.multiple_of(k * own, own), own), cols]

                    @pl.when(here)
                    def _():
                        pltpu.make_async_copy(src, dst, recv2).start()

                    @pl.when(jnp.logical_not(here))
                    def _():
                        pltpu.make_async_remote_copy(
                            src_ref=src,
                            dst_ref=dst,
                            send_sem=send2,
                            recv_sem=recv2,
                            device_id=(target, 2 * g + t // half),
                            device_id_type=MESH,
                        ).start()

        def row_pair(i, _):
            piece(n, 1, 2 * i, 2)
            return 0

        def column_pair(i, _):
            piece(2 * i, 2, n, 1)
            return 0

        lax.fori_loop(0, (n + 1) // 2, row_pair, 0)
        lax.fori_loop(0, n // 2, column_pair, 0)
        piece(n - n % 2, 1, n, 1)
        return 0

    lax.fori_loop(0, tms, phase, 0)
    pltpu.make_async_copy(r_ref, r_ref, recv2).wait()

    pltpu.make_async_copy(x_ref.at[k], x_ref.at[k], send3).wait()
    sent = s_ref.at[pl.ds(0, peers - 1)]
    pltpu.make_async_copy(sent, sent, send1).wait()

    @pl.when(k == t // half)
    def _():
        kept = outs.at[pl.ds(0, tms - 1)]
        pltpu.make_async_copy(kept, kept, send2).wait()

    @pl.when(k != t // half)
    def _():
        pltpu.make_async_copy(outs, outs, send2).wait()


def local(voltages, window):
    tms, freqs = lax.axis_size("tm"), lax.axis_size("freq")
    groups = freqs // 2
    half = tms // 2
    taps, period = window.shape
    antennas, samples = voltages.shape
    spec_here = samples // period
    channels = period // 2
    assert channels == tms * groups
    rows = antennas * 3 // 2
    total = antennas * freqs
    row_count = total // tms
    depth = 2 * spec_here * tms
    result = pl.pallas_call(
        functools.partial(correlate_kernel, tms, groups, (spec_here * tms) ** (-0.5)),
        out_shape=jax.ShapeDtypeStruct((2, half, row_count, total), jnp.bfloat16),
        in_specs=[pl.BlockSpec(memory_space=pl.ANY)] * 3,
        out_specs=pl.BlockSpec(memory_space=pl.ANY),
        scratch_shapes=[
            pltpu.VMEM((antennas, samples + (taps - 1) * period), jnp.bfloat16),
            pltpu.VMEM(window.shape, jnp.float32),
            pltpu.VMEM((4 * channels, period), jnp.bfloat16),
            pltpu.VMEM((period // LANES, antennas * (spec_here // 3 + 1), LANES), jnp.float32),
            pltpu.VMEM((period // LANES, antennas * (2 * spec_here // 3 + 1), LANES), jnp.float32),
            pltpu.VMEM((channels * (rows + 1), LANES), jnp.float32),
            pltpu.VMEM((channels, rows, LANES), jnp.bfloat16),
            pltpu.VMEM((2, half, 2, 2, tms, rows, LANES), jnp.bfloat16),
            pltpu.VMEM((tms, row_count, depth), jnp.bfloat16),
            pltpu.VMEM((tms, 2, row_count // 2, depth), jnp.bfloat16),
            pltpu.VMEM((tms, 2, row_count // 2, total), jnp.bfloat16),
            pltpu.SemaphoreType.DMA((3,)),
            pltpu.SemaphoreType.DMA((2,)),
            pltpu.SemaphoreType.DMA,
            pltpu.SemaphoreType.DMA((tms,)),
            pltpu.SemaphoreType.DMA,
            pltpu.SemaphoreType.DMA,
            pltpu.SemaphoreType.DMA,
            pltpu.SemaphoreType.DMA((tms,)),
        ],
        compiler_params=pltpu.CompilerParams(
            collective_id=0, has_side_effects=True, vmem_limit_bytes=60 << 20
        ),
        cost_estimate=pl.CostEstimate(
            flops=2 * 2 * (total // 2) * total * depth, bytes_accessed=8 << 20, transcendentals=0
        ),
    )(voltages, window, jnp.asarray(dft_table(period, channels)))
    return result.astype(jnp.float32)


def solution(mesh):
    return jax.shard_map(
        local,
        mesh=mesh,
        in_specs=(P("freq", "tm"), P()),
        out_specs=P(None, "freq", "tm", None),
        check_vma=False,
    )
```

time: 83.4 us -> 75.1 us (0.900)
  Pallas kernels: 76.5 us -> 70.1 us
  local copies, waits for them, and re-layouts: 3.05 us -> 0 us
  other arithmetic: 2.48 us -> 4.07 us
    pallas_call x1, Pallas kernels: 76.5 us -> 70.1 us  [local(): pl.pallas_call(functools.partial(correlate_kernel, tms, groups, (spec_her...]
    unnamed x6 -> x0, local copies, waits for them, and re-layouts: 3.05 us -> none
    convert_element_type x1, other arithmetic: 2.48 us -> 4.07 us  [local(): return result.astype(jnp.float32)]
where the time goes in v4:
time: 75.1 us; the launch traced here: 74.2 us
  Pallas kernels  70.1 us (93%)
  other arithmetic  4.07 us (5%)
    pallas_call x1, Pallas kernels, local(): pl.pallas_call(functools.partial(correlate_kernel, tms, groups, (spec_her...  70.1 us
    convert_element_type x1, other arithmetic, local(): return result.astype(jnp.float32)  4.07 us

profile of v4, /device:TPU:24, one launch (start us, length us, event | category | flops | bytes accessed | tf_op | source)
XLA Modules:
  0.0 74.2 jit_solution(5803101943916811485)
XLA Ops:
  0.0 70.1 %shard_map.37 = bf16[2,4,128,1024]{3,2,1,0:T(8,128)(2,1)} custom-call(bf16[32,24576]{1,0:T(8,128)(2,1)} %v_ref.1, f32[8,256]{1,0:T(8,128)} %window_ref.1, bf16[512,256]{1,0:T(8,128)(2,1)} %constant.2.clone.table_ref), custom_call_target="tpu_custom_call" | custom-call | flops 3221225472 | bytes 8388608 | tf_op jit(solution)/shard_map/pallas_call | solution.py:459
  70.1 4.1 %convert_element_type.3 = f32[2,4,128,1024]{3,2,1,0:T(8,128)} convert(bf16[2,4,128,1024]{3,2,1,0:T(8,128)(2,1)} %shard_map.37) | non-fusion elementwise | flops 1048576 | bytes 6291456 | tf_op jit(solution)/shard_map/convert_element_type | solution.py:492

commit v5 on v4

--- a/solution.py
+++ b/solution.py
@@ -314,7 +314,7 @@
     send_phases(EARLY, tms, 0, rows)
 
     wide = tms * LANES
-    lane = lax.broadcasted_iota(jnp.int32, (16, LANES), 1)
+    lane = lax.broadcasted_iota(jnp.int32, (ants, LANES), 1)
     low = lane < LANES // 2
     quarter = lane % (LANES // 2) < LANES // 4
     block = ants * 4
@@ -337,46 +337,43 @@
             device_id=sibling,
             device_id_type=MESH,
         ).start()
-        other = x_ref.at[1 - k, part, high]
-        pltpu.make_async_copy(other, other, recv3.at[n]).wait()
-
-        def assemble(i, _):
-            kk, low_g = i % 2, i // 2
-            base = pl.multiple_of(i * ants, ants)
-            for tt in range(tms):
-                right[n, pl.ds(base, ants), tt * LANES : (tt + 1) * LANES] = x_ref[
-                    kk, part, high, low_g, tt, :ants, :
-                ]
-            for tt in range(0, tms, 2):
-                h0 = x_ref[kk, part, high, low_g, tt, ants:, :].astype(jnp.float32)
-                h1 = x_ref[kk, part, high, low_g, tt + 1, ants:, :].astype(jnp.float32)
-                top = jnp.where(low, h0, pltpu.roll(h1, LANES // 2, 1))
-                bottom = jnp.where(low, pltpu.roll(h0, LANES // 2, 1), h1)
-                cols = slice(wide + tt // 2 * LANES, wide + (tt // 2 + 1) * LANES)
-                right[n, pl.ds(base, ants // 2), cols] = top.astype(jnp.bfloat16)
-                right[n, pl.ds(base + ants // 2, ants // 2), cols] = bottom.astype(jnp.bfloat16)
-            return 0
-
-        lax.fori_loop(0, 4, assemble, 0)
-
-        def swap(i, _):
-            at = pl.multiple_of(i * 16, 16)
-            for tile in range(right.shape[2] // LANES):
-                cols = slice(tile * LANES, (tile + 1) * LANES)
-                kept = right[n, pl.ds(pl.multiple_of(k * own + at, 16), 16), cols]
-                left[n, 0, pl.ds(at, 16), cols] = kept
-                v = kept.astype(jnp.float32)
-                if tile < tms:
+
+        def assemble(kk, mine_too):
+            for low_g in range(2):
+                base = pl.multiple_of((2 * low_g + kk) * ants, ants)
+
+                def put(at, cols, value, turned_value):
+                    count = value.shape[0]
+                    right[n, pl.ds(base + at, count), cols] = value
+                    if mine_too:
+                        left[n, 0, low_g * ants + at : low_g * ants + at + count, cols] = value
+                        left[n, 1, low_g * ants + at : low_g * ants + at + count, cols] = (
+                            turned_value(value)
+                        )
+
+                def turn_wide(v):
                     v = pltpu.roll(v, LANES // 2, 1)
-                    v = jnp.where(low, v, -v)
-                else:
-                    v = jnp.where(
-                        quarter, pltpu.roll(v, LANES - LANES // 4, 1), -pltpu.roll(v, LANES // 4, 1)
-                    )
-                left[n, 1, pl.ds(at, 16), cols] = v.astype(jnp.bfloat16)
-            return 0
-
-        lax.fori_loop(0, own // 16, swap, 0)
+                    return jnp.where(low[: v.shape[0]], v, -v)
+
+                def turn_narrow(v):
+                    ahead = pltpu.roll(v, LANES - LANES // 4, 1)
+                    behind = pltpu.roll(v, LANES // 4, 1)
+                    return jnp.where(quarter[: v.shape[0]], ahead, -behind)
+
+                for tt in range(tms):
+                    cols = slice(tt * LANES, (tt + 1) * LANES)
+                    put(0, cols, x_ref[kk, part, high, low_g, tt, :ants, :], turn_wide)
+                for tt in range(0, tms, 2):
+                    h0 = x_ref[kk, part, high, low_g, tt, ants:, :]
+                    h1 = x_ref[kk, part, high, low_g, tt + 1, ants:, :]
+                    some = low[: ants // 2]
+                    cols = slice(wide + tt // 2 * LANES, wide + (tt // 2 + 1) * LANES)
+                    top = jnp.where(some, h0, pltpu.roll(h1, LANES // 2, 1))
+                    put(0, cols, top, turn_narrow)
+                    bottom = jnp.where(some, pltpu.roll(h0, LANES // 2, 1), h1)
+                    put(ants // 2, cols, bottom, turn_narrow)
+
+        assemble(k, True)
 
         def piece(row, row_count, col, col_count):
             value = lax.dot_general(
@@ -386,7 +383,7 @@
                 preferred_element_type=jnp.float32,
             )
             value = (value * scale).astype(jnp.bfloat16)
-            value = value.reshape(row_count, 2, own, col_count * block)
+            value = value.reshape(row_count, 2, 2, ants, col_count * block)
             for r in range(row_count):
                 to_high, to_part = place(row + r)
                 target = to_high * half + to_part
@@ -394,9 +391,9 @@
                 for c in range(col_count):
                     at_high, at_part = place(col + c)
                     cols = pl.ds(pl.multiple_of((at_high * half + at_part) * block, block), block)
-                    outs[row + r, :, :, cols] = value[r, :, :, c * block : (c + 1) * block]
-                    src = outs.at[row + r, :, :, cols]
-                    dst = r_ref.at[:, slot, pl.ds(pl.multiple_of(k * own, own), own), cols]
+                    outs[row + r, :, :, :, cols] = value[r, :, :, :, c * block : (c + 1) * block]
+                    src = outs.at[row + r, :, :, :, cols]
+                    dst = r_ref.at[:, slot, :, k, :, cols]
 
                     @pl.when(here)
                     def _():
@@ -421,9 +418,21 @@
             piece(2 * i, 2, n, 1)
             return 0
 
-        lax.fori_loop(0, (n + 1) // 2, row_pair, 0)
-        lax.fori_loop(0, n // 2, column_pair, 0)
-        piece(n - n % 2, 1, n, 1)
+        lax.fori_loop(0, n // 2, row_pair, 0)
+
+        @pl.when(n % 2 == 1)
+        def _():
+            piece(n, 1, n - 1, 1)
+
+        other = x_ref.at[1 - k, part, high]
+        pltpu.make_async_copy(other, other, recv3.at[n]).wait()
+        assemble(1 - k, False)
+        lax.fori_loop(0, (n + 1) // 2, column_pair, 0)
+
+        @pl.when(n % 2 == 0)
+        def _():
+            piece(n, 1, n, 1)
+
         return 0
 
     lax.fori_loop(0, tms, phase, 0)
@@ -458,7 +467,7 @@
     depth = 2 * spec_here * tms
     result = pl.pallas_call(
         functools.partial(correlate_kernel, tms, groups, (spec_here * tms) ** (-0.5)),
-        out_shape=jax.ShapeDtypeStruct((2, half, row_count, total), jnp.bfloat16),
+        out_shape=jax.ShapeDtypeStruct((2, half, 2, 2, antennas, total), jnp.bfloat16),
         in_specs=[pl.BlockSpec(memory_space=pl.ANY)] * 3,
         out_specs=pl.BlockSpec(memory_space=pl.ANY),
         scratch_shapes=[
@@ -472,7 +481,7 @@
             pltpu.VMEM((2, half, 2, 2, tms, rows, LANES), jnp.bfloat16),
             pltpu.VMEM((tms, row_count, depth), jnp.bfloat16),
             pltpu.VMEM((tms, 2, row_count // 2, depth), jnp.bfloat16),
-            pltpu.VMEM((tms, 2, row_count // 2, total), jnp.bfloat16),
+            pltpu.VMEM((tms, 2, 2, antennas, total), jnp.bfloat16),
             pltpu.SemaphoreType.DMA((3,)),
             pltpu.SemaphoreType.DMA((2,)),
             pltpu.SemaphoreType.DMA,
@@ -489,7 +498,7 @@
             flops=2 * 2 * (total // 2) * total * depth, bytes_accessed=8 << 20, transcendentals=0
         ),
     )(voltages, window, jnp.asarray(dft_table(period, channels)))
-    return result.astype(jnp.float32)
+    return result.reshape(2, half, row_count, total).astype(jnp.float32)
 
 
 def solution(mesh):

time: 75.1 us -> 73.7 us (0.981)
  Pallas kernels: 70.1 us -> 68.8 us
    pallas_call x1, Pallas kernels: 70.1 us -> 68.8 us  [local(): pl.pallas_call(functools.partial(correlate_kernel, tms, groups, (spec_her...]
where the time goes in v5:
time: 73.7 us; the launch traced here: 72.8 us
  Pallas kernels  68.8 us (93%)
  other arithmetic  4.07 us (6%)
    pallas_call x1, Pallas kernels, local(): pl.pallas_call(functools.partial(correlate_kernel, tms, groups, (spec_her...  68.8 us
    convert_element_type x1, other arithmetic, local(): return result.reshape(2, half, row_count, total).astype(jnp.float32)  4.07 us

profile of v5, /device:TPU:24, one launch (start us, length us, event | category | flops | bytes accessed | tf_op | source)
XLA Modules:
  0.0 72.8 jit_solution(5731647849767133424)
XLA Ops:
  0.0 68.8 %shard_map.37 = bf16[2,4,2,2,32,1024]{5,4,3,2,1,0:T(8,128)(2,1)} custom-call(bf16[32,24576]{1,0:T(8,128)(2,1)} %v_ref.1, f32[8,256]{1,0:T(8,128)} %window_ref.1, bf16[512,256]{1,0:T(8,128)(2,1)} %constant.2.clone.table_ref), custom_call_target="tpu_custom_call" | custom-call | flops 3221225472 | bytes 8388608 | tf_op jit(solution)/shard_map/pallas_call | solution.py:468
  68.8 4.1 %bitcast_convert_fusion = f32[2,4,128,1024]{3,2,1,0:T(8,128)} fusion(bf16[2,4,2,2,32,1024]{5,4,3,2,1,0:T(8,128)(2,1)} %shard_map.37), kind=kLoop, calls=%fused_computation | loop fusion | flops 1048576 | bytes 6291456 | tf_op jit(solution)/shard_map/convert_element_type | solution.py:501

commit v6 on v5

--- a/solution.py
+++ b/solution.py
@@ -450,6 +450,45 @@
     @pl.when(k != t // half)
     def _():
         pltpu.make_async_copy(outs, outs, send2).wait()
+
+
+def cast_kernel(pieces, r_ref, o_ref, taken, wide, read_sems, write_sems):
+    rows = r_ref.shape[0] // pieces
+    slices = [pl.ds(i * rows, rows) for i in range(pieces)]
+    reads = [
+        pltpu.make_async_copy(r_ref.at[some], taken.at[some], read_sems.at[i])
+        for i, some in enumerate(slices)
+    ]
+    writes = [
+        pltpu.make_async_copy(wide.at[some], o_ref.at[some], write_sems.at[i])
+        for i, some in enumerate(slices)
+    ]
+    for read in reads:
+        read.start()
+    for some, read, write in zip(slices, reads, writes):
+        read.wait()
+        wide[some] = taken[some].astype(jnp.float32)
+        write.start()
+    for write in writes:
+        write.wait()
+
+
+def cast(values):
+    pieces = 8
+    anywhere = pl.BlockSpec(memory_space=pl.ANY)
+    return pl.pallas_call(
+        functools.partial(cast_kernel, pieces),
+        out_shape=jax.ShapeDtypeStruct(values.shape, jnp.float32),
+        in_specs=[anywhere],
+        out_specs=anywhere,
+        scratch_shapes=[
+            pltpu.VMEM(values.shape, jnp.bfloat16),
+            pltpu.VMEM(values.shape, jnp.float32),
+            pltpu.SemaphoreType.DMA((pieces,)),
+            pltpu.SemaphoreType.DMA((pieces,)),
+        ],
+        compiler_params=pltpu.CompilerParams(vmem_limit_bytes=60 << 20),
+    )(values)
 
 
 def local(voltages, window):
@@ -498,7 +537,7 @@
             flops=2 * 2 * (total // 2) * total * depth, bytes_accessed=8 << 20, transcendentals=0
         ),
     )(voltages, window, jnp.asarray(dft_table(period, channels)))
-    return result.reshape(2, half, row_count, total).astype(jnp.float32)
+    return cast(result.reshape(2 * half * row_count, total)).reshape(2, half, row_count, total)
 
 
 def solution(mesh):

time: 73.7 us -> 72.8 us (0.988)
  other arithmetic: 4.07 us -> 0 us
  Pallas kernels: 68.8 us -> 71.9 us
    convert_element_type x1 -> x0, other arithmetic: 4.07 us -> none  [local(): return result.reshape(2, half, row_count, total).astype(jnp.float32)]
    pallas_call x0 -> x1, Pallas kernels: none -> 3.12 us  [cast(): pl.pallas_call(functools.partial(cast_kernel, pieces), out_shape=jax.Shap...]
where the time goes in v6:
time: 72.8 us; the launch traced here: 71.9 us
  Pallas kernels  71.9 us (99%)
    pallas_call x1, Pallas kernels, local(): pl.pallas_call(functools.partial(correlate_kernel, tms, groups, (spec_her...  68.8 us
    pallas_call x1, Pallas kernels, cast(): pl.pallas_call(functools.partial(cast_kernel, pieces), out_shape=jax.Shap...  3.12 us

profile of v6, /device:TPU:24, one launch (start us, length us, event | category | flops | bytes accessed | tf_op | source)
XLA Modules:
  0.0 71.9 jit_solution(2275330625574998354)
XLA Ops:
  0.0 68.8 %shard_map.37 = bf16[2,4,2,2,32,1024]{5,4,3,2,1,0:T(8,128)(2,1)} custom-call(bf16[32,24576]{1,0:T(8,128)(2,1)} %v_ref.1, f32[8,256]{1,0:T(8,128)} %window_ref.1, bf16[512,256]{1,0:T(8,128)(2,1)} %constant.2.clone.table_ref), custom_call_target="tpu_custom_call" | custom-call | flops 3221225472 | bytes 8388608 | tf_op jit(solution)/shard_map/pallas_call | solution.py:507
  68.8 3.1 %shard_map.38 = f32[1024,1024]{1,0:T(8,128)} custom-call(bf16[1024,1024]{1,0:T(8,128)(2,1)} %bitcast.2), custom_call_target="tpu_custom_call" | custom-call | tf_op jit(solution)/shard_map/pallas_call | solution.py:479

commit v7 on v6

--- a/solution.py
+++ b/solution.py
@@ -11,7 +11,7 @@
 
 MESH = pl.DeviceIdType.MESH
 LANES = 128
-EARLY = 2
+EARLY = 1
 
 
 def dft_table(length, channels):
@@ -23,14 +23,12 @@
     return np.concatenate([high, low], axis=0)
 
 
-def polyphase(frames, w_ref, tile, first, groups, taps, store, beside=None):
+def polyphase(frames, w_ref, tile, first, groups, taps, store):
     cols = slice(tile * LANES, (tile + 1) * LANES)
     weights = [w_ref[k : k + 1, cols] for k in range(taps)]
 
     def group(i, held):
         held = list(held)
-        if beside is not None:
-            beside(tile * groups + i)
         for u in range(8):
             at = first + i * 8 + u
             held.append(frames(at + taps - 1, tile))
@@ -45,8 +43,7 @@
 
 
 def channelize(
-    v_ref, w_ref, c_ref, s_ref, joined, early, late, turned, loads, halo_sems, t, f, tms, greet, greetings,
-    before, between,
+    v_ref, w_ref, c_ref, s_ref, joined, early, late, turned, loads, halo_sems, t, between
 ):
     taps, period = w_ref.shape
     antennas, samples = v_ref.shape
@@ -78,22 +75,10 @@
     def _():
         joined[:, :halo] = jnp.zeros((antennas, halo), jnp.bfloat16)
 
-    steps = tiles * main // 8
-    each = greetings // 2 // steps
-    lax.fori_loop(0, greetings - each * steps, lambda i, _: greet(i), 0)
     for load in loads:
         load.wait()
     for tile in range(tiles):
-        polyphase(
-            frames,
-            w_ref,
-            tile,
-            first,
-            main // 8,
-            taps,
-            store_main,
-            lambda i: [greet(greetings - 1 - i * each - u) for u in range(each)],
-        )
+        polyphase(frames, w_ref, tile, first, main // 8, taps, store_main)
 
     lane = lax.broadcasted_iota(jnp.int32, (channels, LANES), 1)
     low = lane < LANES // 2
@@ -147,25 +132,11 @@
     for tile in range(tiles):
         polyphase(frames, w_ref, tile, 8, first // 8 - 1, taps, store_rest)
 
-    before()
-    last = joined.at[:, pl.ds(samples, halo)]
-    landing = joined.at[:, pl.ds(0, halo)]
-
-    @pl.when(t < tms - 1)
-    def _():
-        pltpu.make_async_remote_copy(
-            src_ref=last,
-            dst_ref=landing,
-            send_sem=halo_sems.at[0],
-            recv_sem=halo_sems.at[1],
-            device_id=(lax.rem(t + 1, tms), f),
-            device_id_type=MESH,
-        ).start()
-
     between()
 
     @pl.when(t > 0)
     def _():
+        landing = joined.at[:, pl.ds(0, halo)]
         pltpu.make_async_copy(landing, landing, halo_sems.at[1]).wait()
 
     for tile in range(tiles):
@@ -184,10 +155,6 @@
 
     lax.fori_loop(0, eighth // 2, rest_part, 0, unroll=4)
     pack(antennas, paired)
-
-    @pl.when(t < tms - 1)
-    def _():
-        pltpu.make_async_copy(last, last, halo_sems.at[0]).wait()
 
 
 def correlate_kernel(
@@ -209,6 +176,7 @@
     right,
     left,
     outs,
+    ready,
     load_sems,
     halo_sems,
     send1,
@@ -243,19 +211,31 @@
         load.start()
     barrier = pltpu.get_barrier_semaphore()
 
-    def greet(n):
-        tt, gg = lax.rem(t + n // groups, tms), lax.rem(g + n % groups, groups)
-        to = jnp.where(n == 0, 2 * g + 1 - k, 2 * gg + k)
-        pl.semaphore_signal(barrier, inc=1, device_id=(tt, to), device_id_type=MESH)
-        return 0
-
-    for j in range(half):
-        pl.semaphore_signal(
-            barrier, inc=1, device_id=(half * k + j, 2 * g + 1 - k), device_id_type=MESH
-        )
-
-    def await_greetings():
-        pl.semaphore_wait(barrier, peers + jnp.where(k == t // half, 0, tms))
+    def greet(to):
+        pl.semaphore_signal(barrier, inc=1, device_id=to, device_id_type=MESH)
+
+    column = [(lax.rem(t + i, tms), 2 * g + k) for i in range(1, tms)]
+    for i in range(1, groups):
+        greet((t, 2 * lax.rem(g + i, groups) + k))
+    for to in column + [sibling] + [(half * k + j, 2 * g + 1 - k) for j in range(half)]:
+        greet(to)
+    pl.semaphore_wait(barrier, groups + tms - 1 + jnp.where(k == t // half, 0, tms))
+    for to in column:
+        pl.semaphore_signal(ready, inc=1, device_id=to, device_id_type=MESH)
+
+    last = v_ref.at[:, pl.ds(v_ref.shape[1] - halo, halo)]
+    landing = joined.at[:, pl.ds(0, halo)]
+
+    @pl.when(t < tms - 1)
+    def _():
+        pltpu.make_async_remote_copy(
+            src_ref=last,
+            dst_ref=landing,
+            send_sem=halo_sems.at[0],
+            recv_sem=halo_sems.at[1],
+            device_id=(lax.rem(t + 1, tms), f),
+            device_id_type=MESH,
+        ).start()
 
     def send_phase(n, first_row, row_count):
         def send_block(i, _):
@@ -290,6 +270,10 @@
 
     def send_phases(first, last, first_row, row_count):
         lax.fori_loop(first, last, lambda n, _: send_phase(n, first_row, row_count), 0)
+
+    def send_early():
+        pl.semaphore_wait(ready, tms - 1)
+        send_phases(0, EARLY, 0, ants)
 
     channelize(
         v_ref,
@@ -303,12 +287,7 @@
         loads,
         halo_sems,
         t,
-        f,
-        tms,
-        greet,
-        peers,
-        await_greetings,
-        lambda: send_phases(0, EARLY, 0, ants),
+        send_early,
     )
     send_phases(0, EARLY, ants, rows - ants)
     send_phases(EARLY, tms, 0, rows)
@@ -437,6 +416,10 @@
 
     lax.fori_loop(0, tms, phase, 0)
     pltpu.make_async_copy(r_ref, r_ref, recv2).wait()
+
+    @pl.when(t < tms - 1)
+    def _():
+        pltpu.make_async_copy(landing, landing, halo_sems.at[0]).wait()
 
     pltpu.make_async_copy(x_ref.at[k], x_ref.at[k], send3).wait()
     sent = s_ref.at[pl.ds(0, peers - 1)]
@@ -521,6 +504,7 @@
             pltpu.VMEM((tms, row_count, depth), jnp.bfloat16),
             pltpu.VMEM((tms, 2, row_count // 2, depth), jnp.bfloat16),
             pltpu.VMEM((tms, 2, 2, antennas, total), jnp.bfloat16),
+            pltpu.SemaphoreType.REGULAR,
             pltpu.SemaphoreType.DMA((3,)),
             pltpu.SemaphoreType.DMA((2,)),
             pltpu.SemaphoreType.DMA,

time: 72.8 us -> 71.6 us (0.984)
  no operation moved by 1% of the time
where the time goes in v7:
time: 71.6 us; the launch traced here: 71.3 us
  Pallas kernels  71.3 us (100%)
    pallas_call x1, Pallas kernels, local(): pl.pallas_call(functools.partial(correlate_kernel, tms, groups, (spec_her...  68.1 us
    pallas_call x1, Pallas kernels, cast(): pl.pallas_call(functools.partial(cast_kernel, pieces), out_shape=jax.Shap...  3.12 us

profile of v7, /device:TPU:24, one launch (start us, length us, event | category | flops | bytes accessed | tf_op | source)
XLA Modules:
  0.0 71.3 jit_solution(17197344367884570776)
XLA Ops:
  0.0 68.1 %shard_map.37 = bf16[2,4,2,2,32,1024]{5,4,3,2,1,0:T(8,128)(2,1)} custom-call(bf16[32,24576]{1,0:T(8,128)(2,1)} %v_ref.1, f32[8,256]{1,0:T(8,128)} %window_ref.1, bf16[512,256]{1,0:T(8,128)(2,1)} %constant.2.clone.table_ref), custom_call_target="tpu_custom_call" | custom-call | flops 3221225472 | bytes 8388608 | tf_op jit(solution)/shard_map/pallas_call | solution.py:490
  68.1 3.1 %shard_map.38 = f32[1024,1024]{1,0:T(8,128)} custom-call(bf16[1024,1024]{1,0:T(8,128)(2,1)} %bitcast.2), custom_call_target="tpu_custom_call" | custom-call | tf_op jit(solution)/shard_map/pallas_call | solution.py:462

commit v8 on v7

--- a/solution.py
+++ b/solution.py
@@ -127,7 +127,7 @@
             turn(i * 2 + p + paired, jnp.where(low, pltpu.roll(re, LANES // 2, 1), im))
         return 0
 
-    lax.fori_loop(0, paired // 2, main_part, 0, unroll=4)
+    lax.fori_loop(0, paired // 2, main_part, 0, unroll=8)
     pack(0, antennas)
     for tile in range(tiles):
         polyphase(frames, w_ref, tile, 8, first // 8 - 1, taps, store_rest)
@@ -239,7 +239,7 @@
 
     def send_phase(n, first_row, row_count):
         def send_block(i, _):
-            tt = lax.rem(t + i // 2, tms)
+            tt = lax.rem(t + tms + (1 - 2 * k) * (i // 2), tms)
             part = lax.rem(mine + 2 * half - tt % half - n // 2, half)
             high = lax.rem(my_high + tt // half + n % 2, 2)
             gg = (high * half + part) * 2 + lax.rem(g + i, 2)

time: 71.6 us -> 71.2 us (level)
  no operation moved by 1% of the time
where the time goes in v8:
time: 71.2 us; the launch traced here: 70.9 us
  Pallas kernels  70.9 us (100%)
    pallas_call x1, Pallas kernels, local(): pl.pallas_call(functools.partial(correlate_kernel, tms, groups, (spec_her...  67.8 us
    pallas_call x1, Pallas kernels, cast(): pl.pallas_call(functools.partial(cast_kernel, pieces), out_shape=jax.Shap...  3.12 us

profile of v8, /device:TPU:24, one launch (start us, length us, event | category | flops | bytes accessed | tf_op | source)
XLA Modules:
  0.0 70.9 jit_solution(3667372997996525002)
XLA Ops:
  0.0 67.8 %shard_map.37 = bf16[2,4,2,2,32,1024]{5,4,3,2,1,0:T(8,128)(2,1)} custom-call(bf16[32,24576]{1,0:T(8,128)(2,1)} %v_ref.1, f32[8,256]{1,0:T(8,128)} %window_ref.1, bf16[512,256]{1,0:T(8,128)(2,1)} %constant.2.clone.table_ref), custom_call_target="tpu_custom_call" | custom-call | flops 3221225472 | bytes 8388608 | tf_op jit(solution)/shard_map/pallas_call | solution.py:490
  67.8 3.1 %shard_map.38 = f32[1024,1024]{1,0:T(8,128)} custom-call(bf16[1024,1024]{1,0:T(8,128)(2,1)} %bitcast.2), custom_call_target="tpu_custom_call" | custom-call | tf_op jit(solution)/shard_map/pallas_call | solution.py:462

commit v9 on v8

--- a/solution.py
+++ b/solution.py
@@ -75,10 +75,15 @@
     def _():
         joined[:, :halo] = jnp.zeros((antennas, halo), jnp.bfloat16)
 
-    for load in loads:
-        load.wait()
+    window_load, middle, last, table, begin = loads
+    window_load.wait()
+    middle.wait()
     for tile in range(tiles):
-        polyphase(frames, w_ref, tile, first, main // 8, taps, store_main)
+        polyphase(frames, w_ref, tile, first, first // 8, taps, store_main)
+    last.wait()
+    for tile in range(tiles):
+        polyphase(frames, w_ref, tile, 2 * first, first // 8, taps, store_main)
+    table.wait()
 
     lane = lax.broadcasted_iota(jnp.int32, (channels, LANES), 1)
     low = lane < LANES // 2
@@ -129,6 +134,7 @@
 
     lax.fori_loop(0, paired // 2, main_part, 0, unroll=8)
     pack(0, antennas)
+    begin.wait()
     for tile in range(tiles):
         polyphase(frames, w_ref, tile, 8, first // 8 - 1, taps, store_rest)
 
@@ -197,15 +203,15 @@
     my_high = g // (2 * half)
 
     halo = joined.shape[1] - v_ref.shape[1]
+    third = v_ref.shape[1] // 3
+    moves = [(window_ref, w_ref)]
+    for start, stop in ((third - halo, 2 * third), (2 * third, 3 * third), (0, third - halo)):
+        target = joined.at[:, pl.ds(halo + start, stop - start)]
+        moves.append((v_ref.at[:, pl.ds(start, stop - start)], target))
+    moves.insert(3, (table_ref, c_ref))
     loads = [
         pltpu.make_async_copy(source, target, load_sems.at[i])
-        for i, (source, target) in enumerate(
-            (
-                (v_ref, joined.at[:, pl.ds(halo, v_ref.shape[1])]),
-                (window_ref, w_ref),
-                (table_ref, c_ref),
-            )
-        )
+        for i, (source, target) in enumerate(moves)
     ]
     for load in loads:
         load.start()
@@ -239,7 +245,7 @@
 
     def send_phase(n, first_row, row_count):
         def send_block(i, _):
-            tt = lax.rem(t + tms + (1 - 2 * k) * (i // 2), tms)
+            tt = lax.rem(t + i // 2, tms)
             part = lax.rem(mine + 2 * half - tt % half - n // 2, half)
             high = lax.rem(my_high + tt // half + n % 2, 2)
             gg = (high * half + part) * 2 + lax.rem(g + i, 2)
@@ -505,7 +511,7 @@
             pltpu.VMEM((tms, 2, row_count // 2, depth), jnp.bfloat16),
             pltpu.VMEM((tms, 2, 2, antennas, total), jnp.bfloat16),
             pltpu.SemaphoreType.REGULAR,
-            pltpu.SemaphoreType.DMA((3,)),
+            pltpu.SemaphoreType.DMA((5,)),
             pltpu.SemaphoreType.DMA((2,)),
             pltpu.SemaphoreType.DMA,
             pltpu.SemaphoreType.DMA((tms,)),

time: 71.2 us -> 71.3 us (level)
  no operation moved by 1% of the time
where the time goes in v9:
time: 71.3 us; the launch traced here: 71.2 us
  Pallas kernels  71.2 us (100%)
    pallas_call x1, Pallas kernels, local(): pl.pallas_call(functools.partial(correlate_kernel, tms, groups, (spec_her...  68.1 us
    pallas_call x1, Pallas kernels, cast(): pl.pallas_call(functools.partial(cast_kernel, pieces), out_shape=jax.Shap...  3.12 us

profile of v9, /device:TPU:24, one launch (start us, length us, event | category | flops | bytes accessed | tf_op | source)
XLA Modules:
  0.0 71.2 jit_solution(12152173275687418771)
XLA Ops:
  0.0 68.1 %shard_map.37 = bf16[2,4,2,2,32,1024]{5,4,3,2,1,0:T(8,128)(2,1)} custom-call(bf16[32,24576]{1,0:T(8,128)(2,1)} %v_ref.1, f32[8,256]{1,0:T(8,128)} %window_ref.1, bf16[512,256]{1,0:T(8,128)(2,1)} %constant.2.clone.table_ref), custom_call_target="tpu_custom_call" | custom-call | flops 3221225472 | bytes 8388608 | tf_op jit(solution)/shard_map/pallas_call | solution.py:496
  68.1 3.1 %shard_map.38 = f32[1024,1024]{1,0:T(8,128)} custom-call(bf16[1024,1024]{1,0:T(8,128)(2,1)} %bitcast.2), custom_call_target="tpu_custom_call" | custom-call | tf_op jit(solution)/shard_map/pallas_call | solution.py:468
